TPU v7x, 256 devices: a whole 4x4x8 slice. The times are simulated.
256 devices in a mesh: tm: 16 (over y, z_lo, core), dp: 4 (over z_hi), factor: 4 (over x).
Axes of the slice: x: 4, y: 4, z: 8 (z_hi: 4, z_lo: 2; z = z_hi * 2 + z_lo), core: 2. Of those that a mesh axis runs over, the one named last changes fastest.
Arguments:
- activations: bfloat16 [65536, 1280], P(('tm', 'dp'), 'factor'), may hold values from -16 to 16
- gradients: bfloat16 [65536, 2560], P(('tm', 'dp'), 'factor'), may hold values from -16 to 16
- valid_frames: int32 [65536], P(('tm', 'dp')), may hold values from 0 to 1, as said below
- basis_in: bfloat16 [1280, 1280], replicated, may hold values from -0.15625 to 0.15625
- basis_out: bfloat16 [2560, 2560], P(None, 'factor'), may hold values from -0.125 to 0.125
- eigen_in: float32 [1280], replicated, may hold values from 0.01 to 0.3
- eigen_out: float32 [2560], replicated, may hold values from 0.01 to 0.3
- previous_in: float32 [1280, 1280], P(('tm', 'dp', 'factor')), may hold values from -0.6 to 1.5
- previous_out: float32 [2560, 2560], P(('tm', 'dp', 'factor')), may hold values from -0.6 to 1.5
Outputs:
- factor_in: float32 [1280, 1280], P(('tm', 'dp', 'factor'))
- factor_out: float32 [2560, 2560], P(('tm', 'dp', 'factor'))
- preconditioned: bfloat16 [2560, 1280], P(('tm', 'dp', 'factor'))
Inputs may be any that keep to these rules, and one draw needn't show every extreme that they name: `valid_frames`: in each block of 1024 frames, the frames before a drawn length (a third of the block or more) are 1 and the rest 0.
All inputs are finite; a program needn't handle non-finite values.
Results may differ from a plain program's by a relative error of at most 0.009.
Values may be sent and summed in bfloat16 or wider, within the bound.
A program may use at most 128 MiB of HBM per device.

v0:
```python
import jax
import jax.numpy as jnp
from jax import lax
from jax.sharding import PartitionSpec as P

factor_decay = 0.5
damping = 0.001


def frames_product(left, right):
    return lax.dot_general(
        left, right, (((0,), (0,)), ((), ())), preferred_element_type=jnp.float32
    )


def shards(
    activations,
    gradients,
    valid_frames,
    basis_in,
    basis_out,
    eigen_in,
    eigen_out,
    previous_in,
    previous_out,
):
    factor_count = lax.axis_size("factor")
    group_count = lax.axis_size("tm") * lax.axis_size("dp")
    factor_index = lax.axis_index("factor")
    group_index = lax.axis_index("tm") * lax.axis_size("dp") + lax.axis_index("dp")
    weights = valid_frames.astype(jnp.bfloat16)[:, None]
    acts_all, grads_all = (
        lax.all_gather(activations * weights, "factor", axis=1, tiled=True),
        lax.all_gather(gradients * weights, "factor", axis=1, tiled=True),
    )
    frame_count = lax.psum(jnp.sum(valid_frames.astype(jnp.float32)), ("tm", "dp"))
    frames = acts_all.shape[0]
    width_in = acts_all.shape[1]
    width_out = grads_all.shape[1]
    owned_in = width_in // (group_count * factor_count)
    owned_out = width_out // (group_count * factor_count)
    block_out = width_out // factor_count

    def owned(full, row_count):
        shaped = full.reshape(frames, group_count, factor_count, row_count)
        picked = lax.dynamic_index_in_dim(shaped, factor_index, axis=2, keepdims=False)
        return picked.reshape(frames, group_count * row_count)

    picked_in = owned(acts_all, owned_in)
    picked_out = owned(grads_all, owned_out)
    rotated_in = jnp.dot(acts_all, basis_in, preferred_element_type=jnp.float32).astype(
        jnp.bfloat16
    )
    rotated_out = jnp.dot(grads_all, basis_out, preferred_element_type=jnp.float32).astype(
        jnp.bfloat16
    )
    gram_in = lax.psum_scatter(
        frames_product(picked_in, acts_all), ("tm", "dp"), scatter_dimension=0, tiled=True
    )
    rotated = lax.psum_scatter(
        frames_product(rotated_out, rotated_in), ("tm", "dp"), scatter_dimension=0, tiled=True
    )
    gram_out = lax.psum_scatter(
        frames_product(picked_out, grads_all), ("tm", "dp"), scatter_dimension=0, tiled=True
    )
    factor_in = factor_decay * previous_in + (1.0 - factor_decay) * (gram_in / frame_count)
    factor_out = factor_decay * previous_out + (1.0 - factor_decay) * (gram_out / frame_count)
    eigen_rows = lax.dynamic_slice_in_dim(
        eigen_out, factor_index * block_out + group_index * owned_out, owned_out, 0
    )
    scaled = (rotated / frame_count / (eigen_rows[:, None] * eigen_in[None, :] + damping)).astype(
        jnp.bfloat16
    )
    back = lax.dot_general(
        scaled, basis_in, (((1,), (1,)), ((), ())), preferred_element_type=jnp.float32
    ).astype(jnp.bfloat16)
    out_span = width_out // group_count
    out_rows = lax.dynamic_slice_in_dim(basis_out, group_index * out_span, out_span, 0)
    partial_value = jnp.dot(
        out_rows,
        lax.all_gather(back, ("tm", "dp"), axis=0, tiled=True),
        preferred_element_type=jnp.float32,
    )
    preconditioned = lax.psum_scatter(
        partial_value, "factor", scatter_dimension=0, tiled=True
    ).astype(jnp.bfloat16)
    return (factor_in, factor_out, preconditioned)


def solution(mesh):
    in_specs = (
        P(("tm", "dp"), "factor"),
        P(("tm", "dp"), "factor"),
        P(("tm", "dp")),
        P(),
        P(None, "factor"),
        P(),
        P(),
        P(("tm", "dp", "factor"), None),
        P(("tm", "dp", "factor"), None),
    )
    out_specs = (
        P(("tm", "dp", "factor"), None),
        P(("tm", "dp", "factor"), None),
        P(("tm", "dp", "factor"), None),
    )
    return jax.shard_map(shards, mesh=mesh, in_specs=in_specs, out_specs=out_specs, check_vma=False)
```

profile of v0, /device:TPU:1, one launch (start us, length us, event | category | flops | bytes accessed | tf_op | source)
XLA Modules:
  0.0 598.6 jit_solution(4289063502719123167)
XLA Ops:
  7.2 0.8 convert_element_type.21
  8.1 2.1 broadcast_multiply_fusion.1
  10.2 0.0 all-gather.7.cloned.1.call-start
  10.2 2.6 broadcast_multiply_fusion
  12.9 38.9 %all-gather.5.cloned.1.call-done = bf16[1024,1280]{0,1:T(8,128)(2,1)} async-done(((bf16[1024,320]{0,1:T(8,128)(2,1)}), bf16[1024,1280]{0,1:T(8,128)(2,1)}) %all-gather.5.cloned.1.call-update) | async-done | bytes 2621456 | tf_op jit(solution)/shard_map/all_gather | solution.py:33
  51.8 6.0 %reshape.23 = bf16[1024,64,4,5]{0,3,2,1:T(8,128)(2,1)} reshape(bf16[1024,1280]{0,1:T(8,128)(2,1)} %all-gather.5.cloned.1.call-done) | data formatting | bytes 5242880 | tf_op jit(solution)/shard_map/reshape | solution.py:45
  57.9 2.3 constant_dynamic-slice_fusion.1
  60.1 2.1 reshape.24
  62.3 4.2 fusion.17
  66.5 46.8 %all-gather.7.cloned.1.call-done = bf16[1024,2560]{1,0:T(8,128)(2,1)} async-done(((bf16[1024,640]{1,0:T(8,128)(2,1)}), bf16[1024,2560]{1,0:T(8,128)(2,1)}) %all-gather.7.cloned.1.call-update) | async-done | bytes 5242896 | tf_op jit(solution)/shard_map/all_gather | solution.py:34
  113.3 7.9 %copy.13 = bf16[1024,2560]{0,1:T(8,128)(2,1)} copy(bf16[1024,2560]{1,0:T(8,128)(2,1)} %all-gather.7.cloned.1.call-done) | data formatting | bytes 10485760 | tf_op jit(solution)/shard_map/all_gather | solution.py:34
  121.3 10.5 %reshape.25 = bf16[1024,64,4,10]{0,3,2,1:T(8,128)(2,1)} reshape(bf16[1024,2560]{0,1:T(8,128)(2,1)} %copy.13) | data formatting | bytes 10485760 | tf_op jit(solution)/shard_map/reshape | solution.py:45
  131.8 3.2 constant_dynamic-slice_fusion
  135.0 3.6 reshape.26
  138.6 9.3 %fusion.18 = f32[640,2560]{1,0:T(8,128)} fusion(bf16[1024,640]{0,1:T(8,128)(2,1)} %reshape.26, bf16[1024,2560]{1,0:T(8,128)(2,1)} %all-gather.7.cloned.1.call-done), kind=kOutput, calls=%fused_computation.29 | convolution fusion | flops 3355443200 | bytes 13107200 | tf_op jit(solution)/shard_map/dot_general | solution.py:11
  147.9 7.8 %convolution_convert_fusion.2 = bf16[1024,640]{1,0:T(8,128)(2,1)} fusion(bf16[1024,2560]{1,0:T(8,128)(2,1)} %all-gather.7.cloned.1.call-done, bf16[2560,640]{1,0:T(8,128)(2,1)S(1)} %copy-done.5), kind=kOutput, calls=%fused_computation.3 | convolution fusion | flops 3356098560 | bytes 9830400 | tf_op jit(solution)/shard_map/dot_general | solution.py:54
  155.7 11.9 %fusion.1 = f32[640,1280]{1,0:T(8,128)} fusion(bf16[1024,640]{1,0:T(8,128)(2,1)} %convolution_convert_fusion.2, bf16[1024,1280]{0,1:T(8,128)(2,1)} %all-gather.5.cloned.1.call-done, bf16[1280,1280]{1,0:T(8,128)(2,1)S(1)} %copy-done), kind=kOutput, calls=%fused_computation.4 | convolution fusion | flops 5034475520 | bytes 10485760 | tf_op jit(solution)/shard_map/dot_general | solution.py:11
  167.7 0.6 copy-done.3
  168.3 0.6 convert_reduce_fusion
  168.9 128.7 %psum.7 = f32[]{:T(128)} all-reduce(f32[]{:T(128)} %convert_reduce_fusion), channel_id=1, replica_groups=mesh['tm'=16,'dp'=4,'factor'=4] {'tm','dp'}, use_global_device_ids=true, to_apply=%region_2.3 | all-reduce | flops 1 | bytes 8 | tf_op jit(solution)/shard_map/psum | solution.py:36
  297.6 0.8 dynamic_slice.17
  298.4 0.6 dynamic-slice
  299.6 81.2 %all-reduce.8.cloned.1.call-done = (f32[320,1280]{1,0:T(8,128)}, f32[640,2560]{1,0:T(8,128)}, f32[640,1280]{1,0:T(8,128)}) async-done(((f32[320,1280]{1,0:T(8,128)}, f32[640,2560]{1,0:T(8,128)}, f32[640,1280]{1,0:T(8,128)}), (f32[320,1280]{1,0:T(8,128)}, f32[640,2560]{1,0:T(8,128)}, f32[640,1280]{1,0:T(8,128)})) %all-reduce.8.cloned.1.call-update) | async-done | bytes 11468816
  380.8 3.2 fusion
  384.0 0.6 dynamic-slice.6
  385.9 2.1 fusion.9
  388.1 2.3 fusion.3
  390.3 177.1 %all-gather.9.cloned.1.call-done = bf16[64,10,1280]{2,1,0:T(8,128)(2,1)} async-done(((bf16[1,10,1280]{2,1,0:T(8,128)(2,1)}), bf16[64,10,1280]{2,1,0:T(8,128)(2,1)}) %all-gather.9.cloned.1.call-update) | async-done | bytes 1638416 | tf_op jit(solution)/shard_map/all_gather | solution.py:81
  567.4 4.0 reshape.28
  571.4 1.8 fusion.5
  573.2 17.3 %all-reduce.9 = bf16[40,1280]{1,0:T(8,128)(2,1)} all-reduce(f32[40,1280]{1,0:T(8,128)S(1)} %fusion.5), channel_id=5, replica_groups=mesh['tm'=16,'dp'=4,'factor'=4] {'factor'}, use_global_device_ids=true, to_apply=%region_5.6.clone | all-reduce | flops 51200 | bytes 307200
  590.6 1.5 dynamic-slice_convert_fusion
  (22 shorter events, 0.2 us)
Async XLA Ops:
  7.2 148.6 %copy-start = (bf16[1280,1280]{1,0:T(8,128)(2,1)S(1)}, bf16[1280,1280]{1,0:T(8,128)(2,1)}, u32[]{:S(2)}) copy-start(bf16[1280,1280]{1,0:T(8,128)(2,1)} %param.12) | copy-start | bytes 9830404
  7.2 44.7 %all-gather.5.cloned.1.call-start = ((), (), s32[]{:S(2)}) async-start(), calls=%async_computation | async-start | bytes 3276800 | tf_op jit(solution)/shard_map/all_gather | solution.py:33
  10.2 103.2 %all-gather.7.cloned.1.call-start = ((), (), s32[]{:S(2)}) async-start(), calls=%async_computation.1 | async-start | bytes 6553600 | tf_op jit(solution)/shard_map/all_gather | solution.py:34
  12.9 368.0 %all-reduce.8.cloned.1.call-start = ((), (), s32[]{:S(2)}) async-start(), calls=%async_computation.3 | async-start | bytes 22937600
  138.6 9.3 %copy-start.5 = (bf16[2560,640]{1,0:T(8,128)(2,1)S(1)}, bf16[2560,640]{1,0:T(8,128)(2,1)}, u32[]{:S(2)}) copy-start(bf16[2560,640]{1,0:T(8,128)(2,1)} %param.13) | copy-start | bytes 9830404
  167.6 0.7 copy-start.3
  167.6 130.8 %copy-start.7 = (u32[256]{0:T(256)S(1)}, u32[256]{0:T(256)}, u32[]{:S(2)}) copy-start(u32[256]{0:T(256)} %constant.43) | copy-start | bytes 3076
  167.6 213.2 %copy-start.4 = (f32[1280]{0:T(1024)S(1)}, f32[1280]{0:T(1024)}, u32[]{:S(2)}) copy-start(f32[1280]{0:T(1024)} %param.14) | copy-start | bytes 15364
  167.7 216.4 %copy-start.6 = (u32[256]{0:T(256)S(1)}, u32[256]{0:T(256)}, u32[]{:S(2)}) copy-start(u32[256]{0:T(256)} %constant.55) | copy-start | bytes 3076
  167.7 218.2 %copy-start.2 = (f32[5,1280]{1,0:T(8,128)S(1)}, f32[5,1280]{1,0:T(8,128)}, u32[]{:S(2)}) copy-start(f32[5,1280]{1,0:T(8,128)} %param.16) | copy-start | bytes 76804
  167.7 220.4 %copy-start.1 = (f32[10,2560]{1,0:T(8,128)S(1)}, f32[10,2560]{1,0:T(8,128)}, u32[]{:S(2)}) copy-start(f32[10,2560]{1,0:T(8,128)} %param.17) | copy-start | bytes 307204
  167.7 399.7 %all-gather.9.cloned.1.call-start = ((), (), s32[]{:S(2)}) async-start(), calls=%async_computation.2 | async-start | bytes 2662400 | tf_op jit(solution)/shard_map/all_gather | solution.py:81
Sparse Core Ops, SparseCore 0:
  10.3 41.5 all-gather.4
  53.7 59.6 all-gather.6
  167.8 213.0 all-reduce.7
  384.1 183.2 all-gather.8
where the time goes:
time: 607 us; the launch traced here: 599 us
  waiting for transfers between devices  344 us (57%)
  blocking collectives  146 us (24%)
  local copies, waits for them, and re-layouts  43.8 us (7%)
  matrix products  38.2 us (6%)
  between operations  15.8 us (3%)
  other arithmetic  10.6 us (2%)
    all_gather x1, waiting for transfers between devices, shards(): lax.all_gather(back, ('tm', 'dp'), axis=0, tiled=True)  177 us
    psum x1, blocking collectives, shards(): lax.psum(jnp.sum(valid_frames.astype(jnp.float32)), ('tm', 'dp'))  129 us
    unnamed x5, waiting for transfers between devices  81.3 us
    all_gather x1, waiting for transfers between devices, shards(): lax.all_gather(gradients * weights, 'factor', axis=1, tiled=True)  46.8 us
    all_gather x1, waiting for transfers between devices, shards(): lax.all_gather(activations * weights, 'factor', axis=1, tiled=True)  38.9 us
    dot_general x3, matrix products, frames_product(): lax.dot_general(left, right, (((0,), (0,)), ((), ())), preferred_element_...  25.4 us
    unnamed x1, blocking collectives  17.3 us
    reshape x2, local copies, waits for them, and re-layouts, owned(): shaped = full.reshape(frames, group_count, factor_count, row_count)  16.5 us
  transfers between devices with their start and end apart: 4, of which 4 were waited for; matrix products, arithmetic and copies ran while one was open for 4% of the time, Pallas kernels for 0%

commit v1 on v0

v1 whole, which is shorter than its diff:
```python
import functools

import jax
import jax.numpy as jnp
from jax import lax
from jax.experimental import pallas as pl
from jax.experimental.pallas import tpu as pltpu
from jax.sharding import PartitionSpec as P

factor_decay = 0.5
damping = 0.001
MESH = pl.DeviceIdType.MESH
F32 = jnp.float32
BF16 = jnp.bfloat16

FR = 1024
WA = 320
WG = 640
MESSAGES = 128


def device(x, y, z, c):
    return {"tm": y * 4 + (z % 2) * 2 + c, "dp": z // 2, "factor": x}


def dot(left, right):
    return jnp.dot(left, right, preferred_element_type=F32)


def dot_nt(left, right):
    return lax.dot_general(left, right, (((1,), (1,)), ((), ())), preferred_element_type=F32)


def kernel(
    at_ref, g_ref, valid_ref, bi_ref, bo_ref, eo_ref, ei_ref, prev_in_ref, prev_out_ref,
    fin_ref, fout_ref, pre_ref,
    a_all, g_all, gt, bi, bo, bit,
    keep, c_send, c_recv, y_send, y_recv, z_send, z_recv, o_send, o_recv, i_send, i_recv,
    m_keep, mc_send, mc_recv, my_send, my_recv, mz_send, mz_recv, mx, wz, wy, wc,
    st, bt, px_send, px_recv,
    n_c, n_y, n_z, n_total,
    send_sem, recv_sem, load_sem,
):
    tm, dp, x = lax.axis_index("tm"), lax.axis_index("dp"), lax.axis_index("factor")
    y, c = tm // 4, tm % 2
    z = dp * 2 + (tm // 2) % 2
    group = tm * 4 + dp
    unit = group * 4 + x
    left, right, opposite = (x + 3) % 4, (x + 1) % 4, (x + 2) % 4

    def peer(dx=0, dy=0, dz=0, dc=0):
        return device((x + dx) % 4, (y + dy) % 4, (z + dz) % 8, (c + dc) % 2)

    out_unit = 64 * x + 32 * c + 8 * y + z
    out_dst = {"tm": out_unit // 16, "dp": (out_unit // 4) % 4, "factor": out_unit % 4}
    out_src = device(unit // 64, (unit // 8) % 4, unit % 8, (unit // 32) % 2)
    in_unit = [64 * x + 16 * y + 2 * z + h for h in range(2)]
    in_dst = [{"tm": u // 16, "dp": (u // 4) % 4, "factor": u % 4} for u in in_unit]
    in_src = [device(unit // 64, (unit // 16) % 4, (unit // 2) % 8, h) for h in range(2)]

    def same(d):
        return (d["tm"] == tm) & (d["dp"] == dp) & (d["factor"] == x)

    load_bi = pltpu.make_async_copy(bi_ref, bi, load_sem.at[0])
    load_bo = pltpu.make_async_copy(bo_ref, bo, load_sem.at[1])
    load_bi.start()
    load_bo.start()

    barrier = pltpu.get_barrier_semaphore()
    peers = [peer(dx=i) for i in (1, 2, 3)] + [peer(dy=i) for i in (1, 2, 3)]
    peers += [peer(dz=i) for i in range(1, 8)] + [peer(dc=1)]
    for d in peers:
        pl.semaphore_signal(barrier, inc=1, device_id=d, device_id_type=MESH)
    for d in [out_src] + in_src:

        @pl.when(jnp.logical_not(same(d)))
        def _():
            pl.semaphore_signal(barrier, inc=1, device_id=d, device_id_type=MESH)

    expected = len(peers)
    for d in [out_dst] + in_dst:
        expected = expected + jnp.where(same(d), 0, 1)

    length = jnp.sum(valid_ref[...], keepdims=True)
    a_all[x] = jnp.where(
        lax.broadcasted_iota(jnp.int32, (WA, FR), 1) < length, at_ref[...], jnp.zeros((), BF16)
    )
    n_c[0] = jnp.broadcast_to(length.astype(F32), (8, 128))
    pl.semaphore_wait(barrier, expected)

    count = [0]
    started = []

    def fresh():
        count[0] += 1
        return count[0] - 1

    def send(src, dst, to, k):
        copy = pltpu.make_async_remote_copy(
            src_ref=src, dst_ref=dst, send_sem=send_sem.at[k], recv_sem=recv_sem.at[k],
            device_id=to, device_id_type=MESH,
        )
        copy.start()
        started.append(copy)

    def landed(dst, k):
        pltpu.make_async_remote_copy(
            src_ref=dst, dst_ref=dst, send_sem=send_sem.at[k], recv_sem=recv_sem.at[k],
            device_id=peer(dx=1), device_id_type=MESH,
        ).wait_recv()

    class Gather:
        def __init__(self, buf, half):
            self.buf, self.h = buf, half
            self.k = [fresh() for _ in range(6)]

        def part(self, shard, h):
            return self.buf.at[shard, pl.ds(h * self.h, self.h)]

        def open(self):
            own0, own1 = self.part(x, 0), self.part(x, 1)
            send(own0, own0, peer(dx=1), self.k[0])
            send(own1, own1, peer(dx=3), self.k[2])
            send(own1, own1, peer(dx=1), self.k[1])
            send(own0, own0, peer(dx=3), self.k[3])

        def forward(self):
            landed(self.part(left, 0), self.k[0])
            send(self.part(left, 0), self.part(left, 0), peer(dx=1), self.k[4])
            landed(self.part(right, 1), self.k[2])
            send(self.part(right, 1), self.part(right, 1), peer(dx=3), self.k[5])

        def near_left(self):
            landed(self.part(left, 1), self.k[1])

        def near_right(self):
            landed(self.part(right, 0), self.k[3])

        def far(self):
            landed(self.part(opposite, 0), self.k[4])
            landed(self.part(opposite, 1), self.k[5])

    acts = Gather(a_all, WA // 2)
    grads = Gather(g_all, FR // 2)
    acts.open()

    kc, ky, kz = fresh(), [fresh() for _ in range(3)], [fresh() for _ in range(7)]
    send(n_c.at[0], n_c.at[1], peer(dc=1), kc)

    def count_y():
        landed(n_c.at[1], kc)
        n_y[0] = n_c[0] + n_c[1]
        for i in range(3):
            send(n_y.at[0], n_y.at[i + 1], peer(dy=i + 1), ky[i])

    def count_z():
        for i in range(3):
            landed(n_y.at[i + 1], ky[i])
        n_z[0] = n_y[0] + n_y[1] + n_y[2] + n_y[3]
        for i in range(7):
            send(n_z.at[0], n_z.at[i + 1], peer(dz=i + 1), kz[i])

    def count_done():
        for i in range(7):
            landed(n_z.at[i + 1], kz[i])
        total = n_z[0]
        for i in range(7):
            total = total + n_z[i + 1]
        n_total[...] = total

    class Scatter:
        def __init__(self, b):
            self.b = b
            self.kc = fresh()
            self.ky = [fresh() for _ in range(3)]
            self.kz = [fresh() for _ in range(7)]

        def core(self, half):
            b = self.b
            c_send[b] = half(1 - c).astype(BF16)
            send(c_send.at[b], c_recv.at[b], peer(dc=1), self.kc)
            keep[b] = half(c)

        def along_y(self):
            b = self.b
            landed(c_recv.at[b], self.kc)
            total = keep[b] + c_recv[b].astype(F32)
            keep[b] = total
            y_send[b] = total.astype(BF16)
            for i in range(3):
                to = (y + i + 1) % 4
                send(
                    y_send.at[b, pl.ds(pl.multiple_of(to * 80, 16), 80)],
                    y_recv.at[b, i], peer(dy=i + 1), self.ky[i],
                )

        def along_z(self):
            b = self.b
            total = keep[b, pl.ds(pl.multiple_of(y * 80, 16), 80)]
            for i in range(3):
                landed(y_recv.at[b, i], self.ky[i])
                total = total + y_recv[b, i].astype(F32)
            for i in range(8):
                z_send[b, i, :10] = total[10 * i : 10 * i + 10].astype(BF16)
            for i in range(7):
                send(z_send.at[b, (z + i + 1) % 8], z_recv.at[b, i], peer(dz=i + 1), self.kz[i])

        def done(self):
            b = self.b
            total = z_send[b, z].astype(F32)
            for i in range(7):
                landed(z_recv.at[b, i], self.kz[i])
                total = total + z_recv[b, i].astype(F32)
            return total

    blocks = [Scatter(i) for i in range(5)]
    ko = [fresh() for _ in range(4)]
    ki_send = [fresh() for _ in range(2)]
    ki = [fresh() for _ in range(2)]

    def out_copy(i):
        return pltpu.make_async_remote_copy(
            src_ref=o_send.at[i], dst_ref=o_recv.at[i], send_sem=send_sem.at[ko[i]],
            recv_sem=recv_sem.at[ko[i]], device_id=out_dst, device_id_type=MESH,
        )

    def hand_out(i, shard):
        o_send[i] = blocks[i].done()
        self_dst = same(out_dst)

        @pl.when(self_dst)
        def _():
            o_recv[i] = o_send[i]

        @pl.when(jnp.logical_not(self_dst))
        def _():
            out_copy(i).start()

    def in_copy(h):
        return pltpu.make_async_remote_copy(
            src_ref=i_send.at[h], dst_ref=i_recv.at[c], send_sem=send_sem.at[ki_send[h]],
            recv_sem=recv_sem.at[ki[0] + c], device_id=in_dst[h], device_id_type=MESH,
        )

    def hand_in():
        total = blocks[4].done()
        for h in range(2):
            i_send[h, :5] = total[5 * h : 5 * h + 5]
        for h in range(2):
            self_dst = same(in_dst[h])

            @pl.when(self_dst)
            def _(h=h):
                i_recv[c] = i_send[h]

            @pl.when(jnp.logical_not(self_dst))
            def _(h=h):
                in_copy(h).start()

    def out_block(shard):
        def half(h):
            rows = gt[pl.ds(pl.multiple_of(h * 320, 16), 320)]
            return dot(rows, g_all[shard])

        return half

    def in_block(h):
        other = a_all[pl.ds(2 * h, 2)].reshape(2 * WA, FR)
        return dot_nt(a_all[x], other)

    g_all[x] = jnp.where(
        lax.broadcasted_iota(jnp.int32, (FR, WG), 0) < length, g_ref[...], jnp.zeros((), BF16)
    )
    gt[...] = g_all[x].T
    z_send[...] = jnp.zeros_like(z_send)
    mz_send[...] = jnp.zeros_like(mz_send)
    i_send[...] = jnp.zeros_like(i_send)
    px_send[...] = jnp.zeros_like(px_send)
    count_y()
    blocks[0].core(out_block(x))
    count_z()
    acts.forward()
    blocks[0].along_y()
    load_bi.wait()
    bit[...] = bi[...].T
    count_done()
    blocks[0].along_z()
    acts.near_left()
    acts.near_right()
    acts.far()
    grads.open()

    kmc, kmy, kmz = fresh(), [fresh() for _ in range(3)], [fresh() for _ in range(7)]

    def cross(h):
        return dot(a_all[pl.ds(2 * h, 2)].reshape(2 * WA, FR), g_all[x])

    mc_send[...] = cross(1 - c).astype(BF16)
    send(mc_send, mc_recv, peer(dc=1), kmc)
    m_keep[...] = cross(c)
    blocks[4].core(in_block)
    landed(mc_recv, kmc)
    total = m_keep[...] + mc_recv[...].astype(F32)
    m_keep[...] = total
    my_send[...] = total.astype(BF16)
    for i in range(3):
        to = (y + i + 1) % 4
        send(
            my_send.at[pl.ds(pl.multiple_of(to * 160, 16), 160)],
            my_recv.at[i], peer(dy=i + 1), kmy[i],
        )
    hand_out(0, x)
    blocks[4].along_y()
    grads.forward()
    total = m_keep[pl.ds(pl.multiple_of(y * 160, 16), 160)]
    for i in range(3):
        landed(my_recv.at[i], kmy[i])
        total = total + my_recv[i].astype(F32)
    for i in range(8):
        mz_send[i, :20] = total[20 * i : 20 * i + 20].astype(BF16)
    for i in range(7):
        send(mz_send.at[(z + i + 1) % 8], mz_recv.at[i], peer(dz=i + 1), kmz[i])
    blocks[4].along_z()
    total = mz_send[z].astype(F32)
    for i in range(7):
        landed(mz_recv.at[i], kmz[i])
        total = total + mz_recv[i].astype(F32)

    kmx = [fresh() for _ in range(3)]
    mx[x] = total.astype(BF16)
    for i in range(3):
        send(mx.at[x], mx.at[x], peer(dx=i + 1), kmx[i])
    hand_in()
    load_bo.wait()
    for i in range(3):
        landed(mx.at[(x + 3 - i) % 4], kmx[i])
    total = jnp.zeros((32, WG), F32)
    for i in range(4):
        total = total + dot(mx[i], bo[i * WG : (i + 1) * WG])
    kwz, kwy, kwc = [fresh() for _ in range(7)], [fresh() for _ in range(3)], fresh()
    wz[z] = total.astype(BF16)
    for i in range(7):
        send(wz.at[z], wz.at[z], peer(dz=i + 1), kwz[i])

    grads.near_left()
    blocks[1].core(out_block(left))
    for i in range(7):
        landed(wz.at[(z + 7 - i) % 8], kwz[i])
    for i in range(8):
        wy[y, 20 * i : 20 * i + 20] = wz[i, :20]
    for i in range(3):
        send(wy.at[y], wy.at[y], peer(dy=i + 1), kwy[i])
    blocks[1].along_y()
    grads.near_right()
    blocks[2].core(out_block(right))
    for i in range(3):
        landed(wy.at[(y + 3 - i) % 4], kwy[i])
    wc[c] = wy[...].reshape(640, WG)
    send(wc.at[c], wc.at[c], peer(dc=1), kwc)
    blocks[1].along_z()
    blocks[2].along_y()
    landed(wc.at[1 - c], kwc)

    frames = n_total[:1, :1]

    def rotate(t, carry):
        rows = pl.ds(pl.multiple_of(t * 320, 16), 320)
        rotated = dot(bit[rows], wc[...].reshape(2 * 640, WG)) / frames
        st[rows] = (rotated / (ei_ref[rows] * eo_ref[...] + damping)).astype(BF16)
        return carry

    lax.fori_loop(0, 4, rotate, 0)

    def back(t, carry):
        rows = pl.ds(pl.multiple_of(t * 320, 16), 320)
        bt[rows] = dot(bi[rows], st[...]).astype(BF16)
        return carry

    lax.fori_loop(0, 4, back, 0)
    odd = group % 2
    rows = bo[pl.ds(pl.multiple_of(group * 40 - 8 * odd, 16), 48)]
    share = dot_nt(rows, bt[...])
    share = jnp.where(odd == 1, share[8:48], share[:40])
    for i in range(4):
        px_send[i, :10] = share[10 * i : 10 * i + 10].astype(BF16)
    kpx = [fresh() for _ in range(3)]
    for i in range(3):
        send(px_send.at[(x + i + 1) % 4], px_recv.at[i], peer(dx=i + 1), kpx[i])
    blocks[2].along_z()
    hand_out(1, left)
    hand_out(2, right)

    grads.far()
    blocks[3].core(out_block(opposite))
    blocks[3].along_y()
    total = px_send[x].astype(F32)
    for i in range(3):
        landed(px_recv.at[i], kpx[i])
        total = total + px_recv[i].astype(F32)
    pre_ref[...] = total[:10].astype(BF16)
    blocks[3].along_z()

    for h in range(2):

        @pl.when(jnp.logical_not(same(in_src[h])))
        def _(h=h):
            landed(i_recv.at[h], ki[h])

        cols = slice(640 * h, 640 * h + 640)
        fin_ref[:, cols] = factor_decay * prev_in_ref[:, cols] + (1.0 - factor_decay) * (
            i_recv[h, :5] / frames
        )
    hand_out(3, opposite)
    source = unit // 64
    for i, step in enumerate((0, 3, 1, 2)):

        @pl.when(jnp.logical_not(same(out_src)))
        def _(i=i):
            landed(o_recv.at[i], ko[i])

        cols = pl.ds(pl.multiple_of(((source + step) % 4) * WG, 128), WG)
        fout_ref[:, cols] = factor_decay * prev_out_ref[:, cols] + (1.0 - factor_decay) * (
            o_recv[i, :10] / frames
        )

    for copy in started:
        copy.wait_send()
    for i in range(4):

        @pl.when(jnp.logical_not(same(out_dst)))
        def _(i=i):
            out_copy(i).wait_send()

    for h in range(2):

        @pl.when(jnp.logical_not(same(in_dst[h])))
        def _(h=h):
            in_copy(h).wait_send()

    assert count[0] <= MESSAGES


def shards(
    activations, gradients, valid_frames, basis_in, basis_out, eigen_in, eigen_out,
    previous_in, previous_out,
):
    x = lax.axis_index("factor")
    eigen_rows = lax.dynamic_slice_in_dim(eigen_out, x * WG, WG, 0).reshape(1, WG)
    vmem = pl.BlockSpec(memory_space=pltpu.VMEM)
    hbm = pl.BlockSpec(memory_space=pl.ANY)
    V = pltpu.VMEM
    return pl.pallas_call(
        kernel,
        out_shape=(
            jax.ShapeDtypeStruct(previous_in.shape, F32),
            jax.ShapeDtypeStruct(previous_out.shape, F32),
            jax.ShapeDtypeStruct((10, 1280), BF16),
        ),
        in_specs=[vmem, vmem, vmem, hbm, hbm, vmem, vmem, vmem, vmem],
        out_specs=(vmem, vmem, vmem),
        scratch_shapes=[
            V((4, WA, FR), BF16), V((4, FR, WG), BF16), V((WG, FR), BF16),
            V((1280, 1280), BF16), V((2560, WG), BF16), V((1280, 1280), BF16),
            V((5, 320, 640), F32), V((5, 320, 640), BF16), V((5, 320, 640), BF16),
            V((5, 320, 640), BF16), V((5, 3, 80, 640), BF16),
            V((5, 8, 16, 640), BF16), V((5, 7, 16, 640), BF16),
            V((4, 16, 640), F32), V((4, 16, 640), F32),
            V((2, 8, 640), F32), V((2, 8, 640), F32),
            V((640, 640), F32), V((640, 640), BF16), V((640, 640), BF16),
            V((640, 640), BF16), V((3, 160, 640), BF16),
            V((8, 32, 640), BF16), V((7, 32, 640), BF16),
            V((4, 32, 640), BF16), V((8, 32, 640), BF16), V((4, 160, 640), BF16),
            V((2, 640, 640), BF16),
            V((1280, 640), BF16), V((1280, 640), BF16),
            V((4, 16, 1280), BF16), V((3, 16, 1280), BF16),
            V((2, 8, 128), F32), V((4, 8, 128), F32), V((8, 8, 128), F32),
            V((8, 128), F32),
            pltpu.SemaphoreType.DMA((MESSAGES,)), pltpu.SemaphoreType.DMA((MESSAGES,)),
            pltpu.SemaphoreType.DMA((2,)),
        ],
        compiler_params=pltpu.CompilerParams(
            collective_id=0, has_side_effects=True, vmem_limit_bytes=60 * 1024 * 1024
        ),
    )(
        activations.T, gradients, valid_frames.reshape(8, 128), basis_in, basis_out,
        eigen_rows, eigen_in.reshape(1280, 1), previous_in, previous_out,
    )


def solution(mesh):
    rows = P(("tm", "dp", "factor"), None)
    in_specs = (
        P(("tm", "dp"), "factor"),
        P(("tm", "dp"), "factor"),
        P(("tm", "dp")),
        P(),
        P(None, "factor"),
        P(),
        P(),
        rows,
        rows,
    )
    return jax.shard_map(
        shards, mesh=mesh, in_specs=in_specs, out_specs=(rows, rows, rows), check_vma=False
    )
```

time: 607 us -> 156 us (0.26); the launches traced: 599 us -> 156 us
  waiting for transfers between devices: 344 us -> 0 us
  Pallas kernels: 0 us -> 148 us
  blocking collectives: 146 us -> 0 us
  matrix products: 38.2 us -> 0 us
  local copies, waits for them, and re-layouts: 43.8 us -> 7.53 us
  between operations: 15.8 us -> 0.65 us
  other arithmetic: 10.6 us -> 0 us
    all_gather x3 -> x0, waiting for transfers between devices: 263 us -> none  [the longest x1 177 us: shards(): lax.all_gather(back, ('tm', 'dp'), axis=0, tiled=True)]
    pallas_call x0 -> x1, Pallas kernels: none -> 148 us  [shards(): pl.pallas_call(kernel, out_shape=(jax.ShapeDtypeStruct(previous_in.shape,...]
    psum x1 -> x0, blocking collectives: 129 us -> none  [shards(): lax.psum(jnp.sum(valid_frames.astype(jnp.float32)), ('tm', 'dp'))]
    unnamed x5 -> x0, waiting for transfers between devices: 81.3 us -> none
    dot_general x6 -> x0, matrix products: 38.2 us -> none  [the longest x3 25.4 us: frames_product(): lax.dot_general(left, right, (((0,), (0,)), ((), ())), preferred_element_...]
    reshape x4 -> x2, local copies, waits for them, and re-layouts: 22.3 us -> 2.36 us  [the longest x1 1.78 us: shards(): eigen_in.reshape(1280, 1)]
    unnamed x1 -> x0, blocking collectives: 17.3 us -> none
    all_gather x1 -> x0, local copies, waits for them, and re-layouts: 7.94 us -> none  [shards(): lax.all_gather(gradients * weights, 'factor', axis=1, tiled=True)]
  transfers between devices with their start and end apart: 4 -> 0, of which waited for: 4 -> 0; matrix products, arithmetic and copies ran while one was open for 4% -> 0% of each run, Pallas kernels for 0% -> 0%
where the time goes in v1:
time: 156 us
  Pallas kernels  148 us (95%)
  local copies, waits for them, and re-layouts  7.53 us (5%)
    pallas_call x1, Pallas kernels, shards(): pl.pallas_call(kernel, out_shape=(jax.ShapeDtypeStruct(previous_in.shape,...  148 us
    unnamed x3, local copies, waits for them, and re-layouts  4.39 us

profile of v1, /device:TPU:1, one launch (start us, length us, event | category | flops | bytes accessed | tf_op | source)
XLA Modules:
  0.0 156.1 jit_solution(62292467006098265)
XLA Ops:
  0.6 0.8 dynamic_slice.3
  1.4 0.6 reshape.16.eo_ref
  2.0 1.8 %reshape.18.ei_ref = f32[1280,1]{1,0:T(8,128)} reshape(f32[1280]{0:T(1024)} %param.14) | data formatting | bytes 10240 | tf_op jit(solution)/shard_map/reshape | solution.py:486
  3.8 148.0 %shard_map.112 = (f32[5,1280]{1,0:T(8,128)}, f32[10,2560]{1,0:T(8,128)}, bf16[10,1280]{1,0:T(8,128)(2,1)}) custom-call(bf16[320,1024]{1,0:T(8,128)(2,1)} %bitcast.2, bf16[1024,640]{1,0:T(8,128)(2,1)} %g_ref.1, s32[8,128]{1,0:T(8,128)} %bitcast.3, bf16[1280,1280]{1,0:T(8,128)(2,1)} %bi_ref.1, bf16[2560,640]{1,0:T(8,128)(2,1)} %bo_ref.1, ...), custom_call_target="tpu_custom_call" | custom-call | tf_op jit(solution)/shard_map/pallas_call | solution.py:452
  151.7 1.4 copy.16
  153.1 1.6 %copy.17 = f32[10,2560]{1,0:T(8,128)} copy(f32[10,2560]{1,0:T(8,128)} %get-tuple-element.7) | data formatting | bytes 204800
  154.7 1.4 copy.18

commit v2 on v1

v2 whole, which is shorter than its diff:
```python
import functools

import jax
import jax.numpy as jnp
from jax import lax
from jax.experimental import pallas as pl
from jax.experimental.pallas import tpu as pltpu
from jax.sharding import PartitionSpec as P

factor_decay = 0.5
damping = 0.001
MESH = pl.DeviceIdType.MESH
F32 = jnp.float32
BF16 = jnp.bfloat16

FR = 1024
WA = 320
WG = 640
MESSAGES = 128


def device(x, y, z, c):
    return {"tm": y * 4 + (z % 2) * 2 + c, "dp": z // 2, "factor": x}


def dot(left, right):
    return jnp.dot(left, right, preferred_element_type=F32)


def dot_nt(left, right):
    return lax.dot_general(left, right, (((1,), (1,)), ((), ())), preferred_element_type=F32)


def kernel(
    at_ref, g_ref, valid_ref, bi_ref, bo_ref, eo_ref, ei_ref, prev_in_ref, prev_out_ref,
    fin_ref, fout_ref, pre_ref,
    a_all, g_all, gt, bi, bo, bit,
    keep, c_send, c_recv, y_send, y_recv, z_send, z_recv, o_send, o_recv, i_send, i_recv,
    ar_part, ar, bp, m_keep, mc_send, mc_recv, my_send, my_recv, mz_send, mz_recv, mx,
    qx_send, qx_recv, qz_send, qz, qy, qc,
    n_c, n_y, n_z, n_total,
    send_sem, recv_sem, load_sem,
):
    tm, dp, x = lax.axis_index("tm"), lax.axis_index("dp"), lax.axis_index("factor")
    y, c = tm // 4, tm % 2
    z = dp * 2 + (tm // 2) % 2
    group = tm * 4 + dp
    unit = group * 4 + x
    left, right, opposite = (x + 3) % 4, (x + 1) % 4, (x + 2) % 4

    def peer(dx=0, dy=0, dz=0, dc=0):
        return device((x + dx) % 4, (y + dy) % 4, (z + dz) % 8, (c + dc) % 2)

    out_unit = 64 * x + 32 * c + 8 * y + z
    out_dst = {"tm": out_unit // 16, "dp": (out_unit // 4) % 4, "factor": out_unit % 4}
    out_src = device(unit // 64, (unit // 8) % 4, unit % 8, (unit // 32) % 2)
    in_unit = [64 * x + 16 * y + 2 * z + h for h in range(2)]
    in_dst = [{"tm": u // 16, "dp": (u // 4) % 4, "factor": u % 4} for u in in_unit]
    in_src = [device(unit // 64, (unit // 16) % 4, (unit // 2) % 8, h) for h in range(2)]

    def same(d):
        return (d["tm"] == tm) & (d["dp"] == dp) & (d["factor"] == x)

    load_bi = pltpu.make_async_copy(bi_ref, bi, load_sem.at[0])
    load_bo = pltpu.make_async_copy(bo_ref, bo, load_sem.at[1])
    load_bi.start()
    load_bo.start()

    barrier = pltpu.get_barrier_semaphore()
    peers = [peer(dx=i) for i in (1, 2, 3)] + [peer(dy=i) for i in (1, 2, 3)]
    peers += [peer(dz=i) for i in range(1, 8)] + [peer(dc=1)]
    for d in peers:
        pl.semaphore_signal(barrier, inc=1, device_id=d, device_id_type=MESH)
    for d in [out_src] + in_src:

        @pl.when(jnp.logical_not(same(d)))
        def _():
            pl.semaphore_signal(barrier, inc=1, device_id=d, device_id_type=MESH)

    expected = len(peers)
    for d in [out_dst] + in_dst:
        expected = expected + jnp.where(same(d), 0, 1)

    length = jnp.sum(valid_ref[...], keepdims=True)
    a_all[x] = jnp.where(
        lax.broadcasted_iota(jnp.int32, (WA, FR), 1) < length, at_ref[...], jnp.zeros((), BF16)
    )
    n_c[0] = jnp.broadcast_to(length.astype(F32), (8, 128))
    pl.semaphore_wait(barrier, expected)

    count = [0]
    started = []

    def fresh():
        count[0] += 1
        return count[0] - 1

    def send(src, dst, to, k):
        copy = pltpu.make_async_remote_copy(
            src_ref=src, dst_ref=dst, send_sem=send_sem.at[k], recv_sem=recv_sem.at[k],
            device_id=to, device_id_type=MESH,
        )
        copy.start()
        started.append(copy)

    def landed(dst, k):
        pltpu.make_async_remote_copy(
            src_ref=dst, dst_ref=dst, send_sem=send_sem.at[k], recv_sem=recv_sem.at[k],
            device_id=peer(dx=1), device_id_type=MESH,
        ).wait_recv()

    def part(buf, shard, h, cols=None):
        rows = buf.shape[1] // 2
        if cols is None:
            return buf.at[shard, pl.ds(h * rows, rows)]
        return buf.at[shard, pl.ds(h * rows, rows), cols]

    ka = [fresh() for _ in range(6)]
    kg = [fresh() for _ in range(8)]
    near_cols, last_cols = slice(0, 384), slice(384, 640)

    def first(buf, k):
        send(part(buf, x, 0), part(buf, x, 0), peer(dx=1), k[0])
        send(part(buf, x, 1), part(buf, x, 1), peer(dx=3), k[1])

    def second(buf, k):
        send(part(buf, x, 1), part(buf, x, 1), peer(dx=1), k[2])
        send(part(buf, x, 0), part(buf, x, 0), peer(dx=3), k[3])

    def first_landed(buf, k):
        landed(part(buf, left, 0), k[0])
        landed(part(buf, right, 1), k[1])

    def second_landed(buf, k):
        landed(part(buf, left, 1), k[2])
        landed(part(buf, right, 0), k[3])

    def onward(buf, k, cols=None):
        send(part(buf, left, 0, cols), part(buf, left, 0, cols), peer(dx=1), k[0])
        send(part(buf, right, 1, cols), part(buf, right, 1, cols), peer(dx=3), k[1])

    def far_landed(buf, k, cols=None):
        landed(part(buf, opposite, 0, cols), k[0])
        landed(part(buf, opposite, 1, cols), k[1])

    first(a_all, ka)
    second(a_all, ka)

    kc, ky, kz = fresh(), [fresh() for _ in range(3)], [fresh() for _ in range(7)]
    send(n_c.at[0], n_c.at[1], peer(dc=1), kc)

    def count_y():
        landed(n_c.at[1], kc)
        n_y[0] = n_c[0] + n_c[1]
        for i in range(3):
            send(n_y.at[0], n_y.at[i + 1], peer(dy=i + 1), ky[i])

    def count_z():
        for i in range(3):
            landed(n_y.at[i + 1], ky[i])
        n_z[0] = n_y[0] + n_y[1] + n_y[2] + n_y[3]
        for i in range(7):
            send(n_z.at[0], n_z.at[i + 1], peer(dz=i + 1), kz[i])

    def count_done():
        for i in range(7):
            landed(n_z.at[i + 1], kz[i])
        total = n_z[0]
        for i in range(7):
            total = total + n_z[i + 1]
        n_total[...] = total

    class Scatter:
        def __init__(self, b, cols):
            self.b, self.cols = b, cols
            self.kc = fresh()
            self.ky = [fresh() for _ in range(3)]
            self.kz = [fresh() for _ in range(7)]

        def core(self, half):
            b, w = self.b, self.cols
            c_send[b, :, w] = half(1 - c).astype(BF16)
            send(c_send.at[b, :, w], c_recv.at[b, :, w], peer(dc=1), self.kc)
            keep[b, :, w] = half(c)

        def along_y(self):
            b, w = self.b, self.cols
            landed(c_recv.at[b, :, w], self.kc)
            total = keep[b, :, w] + c_recv[b, :, w].astype(F32)
            keep[b, :, w] = total
            y_send[b, :, w] = total.astype(BF16)
            for i in range(3):
                to = (y + i + 1) % 4
                send(
                    y_send.at[b, pl.ds(pl.multiple_of(to * 80, 16), 80), w],
                    y_recv.at[b, i, :, w], peer(dy=i + 1), self.ky[i],
                )

        def along_z(self):
            b, w = self.b, self.cols
            total = keep[b, pl.ds(pl.multiple_of(y * 80, 16), 80), w]
            for i in range(3):
                landed(y_recv.at[b, i, :, w], self.ky[i])
                total = total + y_recv[b, i, :, w].astype(F32)
            for i in range(8):
                z_send[b, i, :10, w] = total[10 * i : 10 * i + 10].astype(BF16)
            for i in range(7):
                send(
                    z_send.at[b, (z + i + 1) % 8, :, w], z_recv.at[b, i, :, w],
                    peer(dz=i + 1), self.kz[i],
                )

        def done(self):
            b, w = self.b, self.cols
            total = z_send[b, z, :, w].astype(F32)
            for i in range(7):
                landed(z_recv.at[b, i, :, w], self.kz[i])
                total = total + z_recv[b, i, :, w].astype(F32)
            return total

    whole = slice(0, 640)
    own_rows, left_rows, right_rows = (Scatter(i, whole) for i in range(3))
    far_rows, last_rows = Scatter(3, near_cols), Scatter(3, last_cols)
    in_rows = Scatter(4, whole)
    out_rows = [own_rows, left_rows, right_rows, far_rows, last_rows]
    ko = [fresh() for _ in out_rows]
    ki_send = [fresh() for _ in range(2)]
    ki = [fresh() for _ in range(2)]

    def out_place(buf, i):
        return buf.at[out_rows[i].b, :, out_rows[i].cols]

    def out_copy(i):
        return pltpu.make_async_remote_copy(
            src_ref=out_place(o_send, i), dst_ref=out_place(o_recv, i),
            send_sem=send_sem.at[ko[i]], recv_sem=recv_sem.at[ko[i]],
            device_id=out_dst, device_id_type=MESH,
        )

    def hand_out(i):
        out_place(o_send, i)[...] = out_rows[i].done()
        self_dst = same(out_dst)

        @pl.when(self_dst)
        def _():
            out_place(o_recv, i)[...] = out_place(o_send, i)[...]

        @pl.when(jnp.logical_not(self_dst))
        def _():
            out_copy(i).start()

    def in_copy(h):
        return pltpu.make_async_remote_copy(
            src_ref=i_send.at[h], dst_ref=i_recv.at[c], send_sem=send_sem.at[ki_send[h]],
            recv_sem=recv_sem.at[ki[0] + c], device_id=in_dst[h], device_id_type=MESH,
        )

    def hand_in():
        total = in_rows.done()
        for h in range(2):
            i_send[h, :5] = total[5 * h : 5 * h + 5]
        for h in range(2):
            self_dst = same(in_dst[h])

            @pl.when(self_dst)
            def _(h=h):
                i_recv[c] = i_send[h]

            @pl.when(jnp.logical_not(self_dst))
            def _(h=h):
                in_copy(h).start()

    def out_block(shard, cols):
        def half(h):
            rows = gt[pl.ds(pl.multiple_of(h * 320, 16), 320)]
            return dot(rows, g_all[shard, :, cols])

        return half

    def in_block(h):
        other = a_all[pl.ds(2 * h, 2)].reshape(2 * WA, FR)
        return dot_nt(a_all[x], other)

    g_all[x] = jnp.where(
        lax.broadcasted_iota(jnp.int32, (FR, WG), 0) < length, g_ref[...], jnp.zeros((), BF16)
    )
    gt[...] = g_all[x].T
    count_y()
    own_rows.core(out_block(x, whole))
    z_send[...] = jnp.zeros_like(z_send)
    mz_send[...] = jnp.zeros_like(mz_send)
    i_send[...] = jnp.zeros_like(i_send)
    count_z()
    first_landed(a_all, ka)
    onward(a_all, ka[4:6])
    first(g_all, kg)
    own_rows.along_y()
    load_bi.wait()
    for i in range(4):
        bit[i] = bi[i * WA : (i + 1) * WA].T
    count_done()
    own_rows.along_z()
    second_landed(a_all, ka)

    def rotate_near(t, carry):
        rows = pl.ds(pl.multiple_of(t * 320, 16), 320)
        total = dot(bit[x, rows], a_all[x]) + dot(bit[left, rows], a_all[left])
        ar_part[rows] = total + dot(bit[right, rows], a_all[right])
        return carry

    lax.fori_loop(0, 4, rotate_near, 0)
    far_landed(a_all, ka[4:6])

    def cross(h):
        def rotate_far(t, carry):
            rows = pl.ds(pl.multiple_of(h * 640 + t * 320, 16), 320)
            ar[rows] = (ar_part[rows] + dot(bit[opposite, rows], a_all[opposite])).astype(BF16)
            return carry

        lax.fori_loop(0, 2, rotate_far, 0)
        return dot(ar[pl.ds(pl.multiple_of(h * 640, 16), 640)], g_all[x])

    kmc, kmy, kmz = fresh(), [fresh() for _ in range(3)], [fresh() for _ in range(7)]
    mc_send[...] = cross(1 - c).astype(BF16)
    send(mc_send, mc_recv, peer(dc=1), kmc)
    m_keep[...] = cross(c)
    second(g_all, kg)
    landed(mc_recv, kmc)
    total = m_keep[...] + mc_recv[...].astype(F32)
    m_keep[...] = total
    my_send[...] = total.astype(BF16)
    for i in range(3):
        to = (y + i + 1) % 4
        send(
            my_send.at[pl.ds(pl.multiple_of(to * 160, 16), 160)],
            my_recv.at[i], peer(dy=i + 1), kmy[i],
        )
    in_rows.core(in_block)
    hand_out(0)

    load_bo.wait()

    def arrange(t, carry):
        to, block = t // 4, t % 4
        line = lax.broadcasted_iota(jnp.int32, (256, WG), 0)
        slot = line % 32
        at_z, second_core = line // 32, jnp.where(slot >= 10, 1, 0)
        source = (at_z % 2) * 320 + (at_z // 2) * 40 + second_core * 150 + slot + to * 10
        chosen = (lax.broadcasted_iota(jnp.int32, (256, WG), 1) == source) & (slot < 20)
        picked = dot(
            chosen.astype(F32).astype(BF16), bo[pl.ds(pl.multiple_of(block * WG, 16), WG)]
        ).astype(BF16)
        for i in range(8):
            rows = pl.ds(pl.multiple_of(i * 128 + block * 32, 32), 32)
            bp[to, rows] = picked[32 * i : 32 * i + 32]
        return carry

    lax.fori_loop(0, 16, arrange, 0)
    total = m_keep[pl.ds(pl.multiple_of(y * 160, 16), 160)]
    for i in range(3):
        landed(my_recv.at[i], kmy[i])
        total = total + my_recv[i].astype(F32)
    for i in range(8):
        mz_send[i, :20] = total[20 * i : 20 * i + 20].astype(BF16)
    for i in range(7):
        send(mz_send.at[(z + i + 1) % 8], mz_recv.at[i], peer(dz=i + 1), kmz[i])
    in_rows.along_y()
    first_landed(g_all, kg)
    total = mz_send[z].astype(F32)
    for i in range(7):
        landed(mz_recv.at[i], kmz[i])
        total = total + mz_recv[i].astype(F32)

    kmx = [fresh() for _ in range(3)]
    mx[x] = total.astype(BF16)
    for i in range(3):
        send(mx.at[x], mx.at[x], peer(dx=i + 1), kmx[i])
    onward(g_all, kg[4:6], near_cols)
    in_rows.along_z()
    frames = n_total[:1, :1]
    row = lax.broadcasted_iota(jnp.int32, (32, 1280), 0) + (c * 640 + y * 160 + z * 20)
    here = lax.broadcasted_iota(jnp.int32, (32, 1280), 1) == row
    eigen_rows = jnp.concatenate([ei_ref[i : i + 1] for i in range(10)], axis=1)
    eigen_rows = jnp.sum(jnp.where(here, eigen_rows, 0.0), axis=1, keepdims=True)
    eigen_cols = jnp.concatenate([eo_ref[pl.ds(5 * x + i, 1)] for i in range(5)], axis=1)
    for i in range(3):
        landed(mx.at[(x + 3 - i) % 4], kmx[i])
    total = jnp.zeros((32, WG), F32)
    for i in range(4):
        total = total + dot(mx[i], bo[i * WG : (i + 1) * WG])
    scaled = (total / frames / (eigen_rows * eigen_cols + damping)).astype(BF16)
    kqx, kqz = [fresh() for _ in range(3)], [fresh() for _ in range(7)]
    kqy, kqc = [fresh() for _ in range(3)], fresh()
    for i in range(4):
        qx_send[i] = dot_nt(scaled, bp[i]).astype(BF16)
    for i in range(3):
        send(qx_send.at[(x + i + 1) % 4], qx_recv.at[i], peer(dx=i + 1), kqx[i])
    onward(g_all, kg[6:8], last_cols)
    second_landed(g_all, kg)
    left_rows.core(out_block(left, whole))
    hand_in()
    total = qx_send[x].astype(F32)
    for i in range(3):
        landed(qx_recv.at[i], kqx[i])
        total = total + qx_recv[i].astype(F32)
    for i in range(8):
        qz_send[i] = total[:, 128 * i : 128 * i + 128].astype(BF16)
    qz[z] = qz_send[z]
    for i in range(7):
        send(qz_send.at[(z + i + 1) % 8], qz.at[z], peer(dz=i + 1), kqz[i])
    left_rows.along_y()
    right_rows.core(out_block(right, whole))
    for i in range(7):
        landed(qz.at[(z + 7 - i) % 8], kqz[i])
    for i in range(8):
        qy[y, 20 * i : 20 * i + 20] = qz[i, :20]
    for i in range(3):
        send(qy.at[y], qy.at[y], peer(dy=i + 1), kqy[i])
    right_rows.along_y()
    left_rows.along_z()
    for i in range(3):
        landed(qy.at[(y + 3 - i) % 4], kqy[i])
    qc[c] = qy[...].reshape(640, 128)
    send(qc.at[c], qc.at[c], peer(dc=1), kqc)
    far_landed(g_all, kg[4:6], near_cols)
    far_rows.core(out_block(opposite, near_cols))
    right_rows.along_z()
    far_rows.along_y()
    landed(qc.at[1 - c], kqc)
    mine = lax.broadcasted_iota(jnp.int32, (16, 128), 0) + (y * 32 + c * 10)
    mine = lax.broadcasted_iota(jnp.int32, (16, 128), 1) == mine
    picked = dot_nt(mine.astype(F32).astype(BF16), qc[...].reshape(1280, 128)).astype(BF16)
    pre_ref[...] = dot_nt(picked, bi[...])[:10].astype(BF16)
    hand_out(1)

    far_landed(g_all, kg[6:8], last_cols)
    last_rows.core(out_block(opposite, last_cols))
    far_rows.along_z()
    last_rows.along_y()
    hand_out(2)
    last_rows.along_z()
    hand_out(3)

    for h in range(2):

        @pl.when(jnp.logical_not(same(in_src[h])))
        def _(h=h):
            landed(i_recv.at[h], ki[h])

        cols = slice(640 * h, 640 * h + 640)
        fin_ref[:, cols] = factor_decay * prev_in_ref[:, cols] + (1.0 - factor_decay) * (
            i_recv[h, :5] / frames
        )
    hand_out(4)
    source = unit // 64
    for i, step in enumerate((0, 3, 1, 2, 2)):

        @pl.when(jnp.logical_not(same(out_src)))
        def _(i=i):
            landed(out_place(o_recv, i), ko[i])

        w = out_rows[i].cols
        cols = pl.ds(pl.multiple_of(((source + step) % 4) * WG, 128) + w.start, w.stop - w.start)
        fout_ref[:, cols] = factor_decay * prev_out_ref[:, cols] + (1.0 - factor_decay) * (
            o_recv[out_rows[i].b, :10, w] / frames
        )

    for copy in started:
        copy.wait_send()
    for i in range(5):

        @pl.when(jnp.logical_not(same(out_dst)))
        def _(i=i):
            out_copy(i).wait_send()

    for h in range(2):

        @pl.when(jnp.logical_not(same(in_dst[h])))
        def _(h=h):
            in_copy(h).wait_send()

    assert count[0] <= MESSAGES


def shards(
    activations, gradients, valid_frames, basis_in, basis_out, eigen_in, eigen_out,
    previous_in, previous_out,
):
    vmem = pl.BlockSpec(memory_space=pltpu.VMEM)
    hbm = pl.BlockSpec(memory_space=pl.ANY)
    V = pltpu.VMEM
    return pl.pallas_call(
        kernel,
        out_shape=(
            jax.ShapeDtypeStruct(previous_in.shape, F32),
            jax.ShapeDtypeStruct(previous_out.shape, F32),
            jax.ShapeDtypeStruct((10, 1280), BF16),
        ),
        in_specs=[vmem, vmem, vmem, hbm, hbm, vmem, vmem, vmem, vmem],
        out_specs=(vmem, vmem, vmem),
        scratch_shapes=[
            V((4, WA, FR), BF16), V((4, FR, WG), BF16), V((WG, FR), BF16),
            V((1280, 1280), BF16), V((2560, WG), BF16), V((4, 1280, WA), BF16),
            V((5, 320, 640), F32), V((5, 320, 640), BF16), V((5, 320, 640), BF16),
            V((5, 320, 640), BF16), V((5, 3, 80, 640), BF16),
            V((5, 8, 16, 640), BF16), V((5, 7, 16, 640), BF16),
            V((4, 16, 640), F32), V((4, 16, 640), F32),
            V((2, 8, 640), F32), V((2, 8, 640), F32),
            V((1280, FR), F32), V((1280, FR), BF16), V((4, 1024, WG), BF16),
            V((640, 640), F32), V((640, 640), BF16), V((640, 640), BF16),
            V((640, 640), BF16), V((3, 160, 640), BF16),
            V((8, 32, 640), BF16), V((7, 32, 640), BF16),
            V((4, 32, 640), BF16),
            V((4, 32, 1024), BF16), V((3, 32, 1024), BF16), V((8, 32, 128), BF16),
            V((8, 32, 128), BF16), V((4, 160, 128), BF16), V((2, 640, 128), BF16),
            V((2, 8, 128), F32), V((4, 8, 128), F32), V((8, 8, 128), F32),
            V((8, 128), F32),
            pltpu.SemaphoreType.DMA((MESSAGES,)), pltpu.SemaphoreType.DMA((MESSAGES,)),
            pltpu.SemaphoreType.DMA((2,)),
        ],
        compiler_params=pltpu.CompilerParams(
            collective_id=0, has_side_effects=True, vmem_limit_bytes=60 * 1024 * 1024
        ),
    )(
        activations.T, gradients, valid_frames.reshape(8, 128), basis_in, basis_out,
        eigen_out.reshape(20, 128), eigen_in.reshape(10, 128), previous_in, previous_out,
    )


def solution(mesh):
    rows = P(("tm", "dp", "factor"), None)
    in_specs = (
        P(("tm", "dp"), "factor"),
        P(("tm", "dp"), "factor"),
        P(("tm", "dp")),
        P(),
        P(None, "factor"),
        P(),
        P(),
        rows,
        rows,
    )
    return jax.shard_map(
        shards, mesh=mesh, in_specs=in_specs, out_specs=(rows, rows, rows), check_vma=False
    )
```

time: 156 us -> 119 us (0.76)
  Pallas kernels: 148 us -> 113 us
  local copies, waits for them, and re-layouts: 7.53 us -> 4.39 us
    pallas_call x1, Pallas kernels: 148 us -> 113 us  [shards(): pl.pallas_call(kernel, out_shape=(jax.ShapeDtypeStruct(previous_in.shape,...]
    reshape x2 -> x0, local copies, waits for them, and re-layouts: 2.36 us -> none  [the longest x1 1.78 us: shards(): eigen_in.reshape(1280, 1)]
where the time goes in v2:
time: 119 us; the launch traced here: 118 us
  Pallas kernels  113 us (95%)
  local copies, waits for them, and re-layouts  4.39 us (4%)
    pallas_call x1, Pallas kernels, shards(): pl.pallas_call(kernel, out_shape=(jax.ShapeDtypeStruct(previous_in.shape,...  113 us
    unnamed x3, local copies, waits for them, and re-layouts  4.39 us

profile of v2, /device:TPU:1, one launch (start us, length us, event | category | flops | bytes accessed | tf_op | source)
XLA Modules:
  0.0 117.7 jit_solution(6648044330652991521)
XLA Ops:
  0.6 112.7 %shard_map.112 = (f32[5,1280]{1,0:T(8,128)}, f32[10,2560]{1,0:T(8,128)}, bf16[10,1280]{1,0:T(8,128)(2,1)}) custom-call(bf16[320,1024]{1,0:T(8,128)(2,1)} %bitcast.4, bf16[1024,640]{1,0:T(8,128)(2,1)} %g_ref.1, s32[8,128]{1,0:T(8,128)} %bitcast.7, bf16[1280,1280]{1,0:T(8,128)(2,1)} %bi_ref.1, bf16[2560,640]{1,0:T(8,128)(2,1)} %bo_ref.1, f32[20,128]{1,0:T(8,128)} %bitcast.5, ...), custom_call_target="tpu_custom_call" | custom-call | tf_op jit(solution)/shard_map/pallas_call | solution.py:492
  113.3 1.4 %copy.15 = f32[5,1280]{1,0:T(8,128)} copy(f32[5,1280]{1,0:T(8,128)} %get-tuple-element.6) | data formatting | bytes 51200
  114.7 1.6 %copy.16 = f32[10,2560]{1,0:T(8,128)} copy(f32[10,2560]{1,0:T(8,128)} %get-tuple-element.7) | data formatting | bytes 204800
  116.3 1.4 %copy.17 = bf16[10,1280]{1,0:T(8,128)(2,1)} copy(bf16[10,1280]{1,0:T(8,128)(2,1)} %get-tuple-element.8) | data formatting | bytes 51200

commit v3 on v2

v3 whole, which is shorter than its diff:
```python
import functools

import jax
import jax.numpy as jnp
from jax import lax
from jax.experimental import pallas as pl
from jax.experimental.pallas import tpu as pltpu
from jax.sharding import PartitionSpec as P

factor_decay = 0.5
damping = 0.001
MESH = pl.DeviceIdType.MESH
F32 = jnp.float32
BF16 = jnp.bfloat16

FR = 1024
WA = 320
WG = 640
MESSAGES = 144


def device(x, y, z, c):
    return {"tm": y * 4 + (z % 2) * 2 + c, "dp": z // 2, "factor": x}


def dot(left, right):
    return jnp.dot(left, right, preferred_element_type=F32)


def dot_nt(left, right):
    return lax.dot_general(left, right, (((1,), (1,)), ((), ())), preferred_element_type=F32)


WIDTHS = (640, 640, 768, 512, 384, 256)


def lines_of(width):
    return (10 * (width // 128) + 15) // 16 * 16


def kernel(
    at_ref, g_ref, valid_ref, bi_ref, bo_ref, eo_ref, ei_ref, prev_in_ref, prev_out_ref,
    fin_ref, fout_ref, pre_ref,
    a_all, g_all, gt, bi, bo, bit,
    keeps, c_sends, c_recvs, y_sends, y_recvs, z_sends, z_recvs, o_sends, o_recvs, i_send, i_recv,
    ar_part, ar, chosen, g_raw, m_keep, mc_send, mc_recv, my_send, my_recv, mz_send, mz_recv, mx,
    qx_send, qx_recv, qz_send, qz, qy, qc,
    n_c, n_y, n_z, n_total,
    send_sem, recv_sem, load_sem,
):
    tm, dp, x = lax.axis_index("tm"), lax.axis_index("dp"), lax.axis_index("factor")
    y, c = tm // 4, tm % 2
    z = dp * 2 + (tm // 2) % 2
    group = tm * 4 + dp
    unit = group * 4 + x
    left, right, opposite = (x + 3) % 4, (x + 1) % 4, (x + 2) % 4

    def peer(dx=0, dy=0, dz=0, dc=0):
        return device((x + dx) % 4, (y + dy) % 4, (z + dz) % 8, (c + dc) % 2)

    turn_dsts = [device(i, x, z, c) for i in range(4)]
    turn_srcs = [device(y, i, z, c) for i in range(4)]
    own_unit = 64 * x + 32 * c + 8 * y + z
    out_dst = {"tm": own_unit // 16, "dp": (own_unit // 4) % 4, "factor": own_unit % 4}
    out_src = device(unit // 64, (unit // 8) % 4, unit % 8, (unit // 32) % 2)
    in_unit = [64 * x + 16 * y + 2 * z + h for h in range(2)]
    in_dst = [{"tm": u // 16, "dp": (u // 4) % 4, "factor": u % 4} for u in in_unit]
    in_src = [device(unit // 64, (unit // 16) % 4, (unit // 2) % 8, h) for h in range(2)]

    def same(d):
        return (d["tm"] == tm) & (d["dp"] == dp) & (d["factor"] == x)

    load_bi = pltpu.make_async_copy(bi_ref, bi, load_sem.at[0])
    load_bo = pltpu.make_async_copy(bo_ref, bo, load_sem.at[1])
    load_g = pltpu.make_async_copy(g_ref, g_raw, load_sem.at[2])
    load_g.start()
    load_bi.start()
    load_bo.start()

    barrier = pltpu.get_barrier_semaphore()
    peers = [peer(dx=i) for i in (1, 2, 3)] + [peer(dy=i) for i in (1, 2, 3)]
    peers += [peer(dz=i) for i in range(1, 8)] + [peer(dc=1)]
    for d in peers:
        pl.semaphore_signal(barrier, inc=1, device_id=d, device_id_type=MESH)
    for d in turn_srcs + [out_src] + in_src:

        @pl.when(jnp.logical_not(same(d)))
        def _():
            pl.semaphore_signal(barrier, inc=1, device_id=d, device_id_type=MESH)

    expected = len(peers)
    for d in turn_dsts + [out_dst] + in_dst:
        expected = expected + jnp.where(same(d), 0, 1)

    length = jnp.sum(valid_ref[...], keepdims=True)
    a_all[x] = jnp.where(
        lax.broadcasted_iota(jnp.int32, (WA, FR), 1) < length, at_ref[...], jnp.zeros((), BF16)
    )
    n_c[0] = jnp.broadcast_to(length.astype(F32), (8, 128))
    mx[x] = jnp.zeros((32, WG), BF16)
    qz_send[...] = jnp.zeros_like(qz_send)
    pl.semaphore_wait(barrier, expected)

    count = [0]
    started = []

    def fresh():
        count[0] += 1
        return count[0] - 1

    def send(src, dst, to, k):
        copy = pltpu.make_async_remote_copy(
            src_ref=src, dst_ref=dst, send_sem=send_sem.at[k], recv_sem=recv_sem.at[k],
            device_id=to, device_id_type=MESH,
        )
        copy.start()
        started.append(copy)

    def landed(dst, k):
        pltpu.make_async_remote_copy(
            src_ref=dst, dst_ref=dst, send_sem=send_sem.at[k], recv_sem=recv_sem.at[k],
            device_id=peer(dx=1), device_id_type=MESH,
        ).wait_recv()

    def part(buf, shard, h, cols=None):
        rows = buf.shape[1] // 2
        rows = pl.ds(0, buf.shape[1]) if h is None else pl.ds(h * rows, rows)
        return buf.at[shard, rows] if cols is None else buf.at[shard, rows, cols]

    ka = [fresh() for _ in range(6)]
    kg = [fresh() for _ in range(8)]
    near_cols, last_cols = slice(0, 384), slice(384, 640)

    def both(buf, k, to_right, to_left, cols=None):
        for shard, h, i in ((x, to_right, 1), (x, to_left, 3)):
            at = part(buf, shard, h, cols)
            send(at, at, peer(dx=i), k[i // 2])

    def both_landed(buf, k, from_left, from_right, cols=None):
        landed(part(buf, left, from_left, cols), k[0])
        landed(part(buf, right, from_right, cols), k[1])

    def onward(buf, k, cols=None):
        send(part(buf, left, 0, cols), part(buf, left, 0, cols), peer(dx=1), k[0])
        send(part(buf, right, 1, cols), part(buf, right, 1, cols), peer(dx=3), k[1])

    def far_landed(buf, k, cols=None):
        landed(part(buf, opposite, 0, cols), k[0])
        landed(part(buf, opposite, 1, cols), k[1])

    both(a_all, ka[0:2], 0, 1)
    both(a_all, ka[2:4], 1, 0)

    kc, ky, kz = fresh(), [fresh() for _ in range(3)], [fresh() for _ in range(7)]
    send(n_c.at[0], n_c.at[1], peer(dc=1), kc)

    def count_y():
        landed(n_c.at[1], kc)
        n_y[0] = n_c[0] + n_c[1]
        for i in range(3):
            send(n_y.at[0], n_y.at[i + 1], peer(dy=i + 1), ky[i])

    def count_z():
        for i in range(3):
            landed(n_y.at[i + 1], ky[i])
        n_z[0] = n_y[0] + n_y[1] + n_y[2] + n_y[3]
        for i in range(7):
            send(n_z.at[0], n_z.at[i + 1], peer(dz=i + 1), kz[i])

    def count_done():
        for i in range(7):
            landed(n_z.at[i + 1], kz[i])
        total = n_z[0]
        for i in range(7):
            total = total + n_z[i + 1]
        n_total[...] = total

    class Scatter:
        def __init__(self, b):
            self.tiles = WIDTHS[b] // 128
            self.keep, self.c_send, self.c_recv = keeps[b], c_sends[b], c_recvs[b]
            self.y_send, self.y_recv = y_sends[b], y_recvs[b]
            self.z_send, self.z_recv = z_sends[b], z_recvs[b]
            self.o_send, self.o_recv = o_sends[b], o_recvs[b]
            self.kc, self.ko = fresh(), fresh()
            self.ky = [fresh() for _ in range(3)]
            self.kz = [fresh() for _ in range(7)]

        def core(self, half):
            self.c_send[...] = half(1 - c).astype(BF16)
            send(self.c_send, self.c_recv, peer(dc=1), self.kc)
            self.keep[...] = half(c)

        def along_y(self):
            landed(self.c_recv, self.kc)
            total = self.keep[...] + self.c_recv[...].astype(F32)
            self.keep[...] = total
            self.y_send[...] = total.astype(BF16)
            for i in range(3):
                to = (y + i + 1) % 4
                send(
                    self.y_send.at[pl.ds(pl.multiple_of(to * 80, 16), 80)],
                    self.y_recv.at[i], peer(dy=i + 1), self.ky[i],
                )

        def sum_y(self):
            total = self.keep[pl.ds(pl.multiple_of(y * 80, 16), 80)]
            for i in range(3):
                landed(self.y_recv.at[i], self.ky[i])
                total = total + self.y_recv[i].astype(F32)
            return total

        def along_z(self):
            total = self.sum_y()
            for i in range(8):
                pieces = [
                    total[10 * i : 10 * i + 10, 128 * j : 128 * j + 128] for j in range(self.tiles)
                ]
                pieces = jnp.concatenate(pieces, axis=0).astype(BF16)
                self.z_send[i, : 10 * self.tiles] = pieces
            for i in range(7):
                send(
                    self.z_send.at[(z + i + 1) % 8], self.z_recv.at[i],
                    peer(dz=i + 1), self.kz[i],
                )

        def done(self):
            total = self.z_send[z].astype(F32)
            for i in range(7):
                landed(self.z_recv.at[i], self.kz[i])
                total = total + self.z_recv[i].astype(F32)
            return total

        def out_copy(self):
            return pltpu.make_async_remote_copy(
                src_ref=self.o_send, dst_ref=self.o_recv, send_sem=send_sem.at[self.ko],
                recv_sem=recv_sem.at[self.ko], device_id=out_dst, device_id_type=MESH,
            )

        def hand_out(self):
            self.o_send[...] = self.done()
            self_dst = same(out_dst)

            @pl.when(self_dst)
            def _():
                self.o_recv[...] = self.o_send[...]

            @pl.when(jnp.logical_not(self_dst))
            def _():
                self.out_copy().start()

        def handed_out(self):
            @pl.when(jnp.logical_not(same(out_src)))
            def _():
                landed(self.o_recv, self.ko)

            return self.o_recv[...]

    class Turned(Scatter):
        def __init__(self, b):
            super().__init__(b)
            self.k_send, self.k = [fresh() for _ in range(4)], [fresh() for _ in range(4)]

        def copy(self, i):
            return pltpu.make_async_remote_copy(
                src_ref=self.y_send.at[pl.ds(80 * i, 80)], dst_ref=self.y_recv.at[y],
                send_sem=send_sem.at[self.k_send[i]], recv_sem=recv_sem.at[self.k[0] + y],
                device_id=turn_dsts[i], device_id_type=MESH,
            )

        def along_y(self):
            landed(self.c_recv, self.kc)
            total = self.keep[...] + self.c_recv[...].astype(F32)
            for i in range(4):
                starts = [(j % 2) * 160 + (j // 2) * 40 + 10 * i for j in range(8)]
                pieces = [total[start : start + 10] for start in starts]
                self.y_send[80 * i : 80 * i + 80] = jnp.concatenate(pieces, axis=0).astype(BF16)
            for i in range(4):
                self_dst = same(turn_dsts[i])

                @pl.when(self_dst)
                def _(i=i):
                    self.y_recv[y] = self.y_send[80 * i : 80 * i + 80]

                @pl.when(jnp.logical_not(self_dst))
                def _(i=i):
                    self.copy(i).start()

        def sum_y(self):
            total = jnp.zeros((80, 128 * self.tiles), F32)
            for i in range(4):

                @pl.when(jnp.logical_not(same(turn_srcs[i])))
                def _(i=i):
                    landed(self.y_recv.at[i], self.k[i])

                total = total + self.y_recv[i].astype(F32)
            return total

    in_rows, own_rows, near_rows, second_rows, far_rows = (Scatter(i) for i in range(5))
    last_rows = Turned(5)
    ki_send = [fresh() for _ in range(2)]
    ki = [fresh() for _ in range(2)]

    def in_copy(h):
        return pltpu.make_async_remote_copy(
            src_ref=i_send.at[h], dst_ref=i_recv.at[c], send_sem=send_sem.at[ki_send[h]],
            recv_sem=recv_sem.at[ki[0] + c], device_id=in_dst[h], device_id_type=MESH,
        )

    def hand_in():
        total = in_rows.done()
        for h in range(2):
            for j in range(5):
                lanes = slice(128 * j, 128 * j + 128)
                i_send[h, :5, lanes] = total[10 * j + 5 * h : 10 * j + 5 * h + 5]
        for h in range(2):
            self_dst = same(in_dst[h])

            @pl.when(self_dst)
            def _(h=h):
                i_recv[c] = i_send[h]

            @pl.when(jnp.logical_not(self_dst))
            def _(h=h):
                in_copy(h).start()

    def own_half(h):
        return dot(gt[pl.ds(pl.multiple_of(h * 320, 16), 320)], g_all[x])

    def near_half(cols):
        def half(h):
            rows = gt[pl.ds(pl.multiple_of(h * 320, 16), 320)]
            sides = [dot(rows, g_all[shard, :, cols]) for shard in (left, right)]
            return jnp.concatenate(sides, axis=1)

        return half

    def far_half(h):
        rows = gt[pl.ds(pl.multiple_of(h * 320, 16), 320)]
        return dot(rows, g_all[opposite, :, near_cols])

    def last_half(h):
        rows = [gt[pl.ds(pl.multiple_of(i * 320 + h * 160, 16), 160)] for i in range(2)]
        return dot(jnp.concatenate(rows, axis=0), g_all[opposite, :, last_cols])

    def in_block(h):
        other = a_all[pl.ds(2 * h, 2)].reshape(2 * WA, FR)
        return dot_nt(a_all[x], other)

    load_g.wait()
    g_all[x] = jnp.where(
        lax.broadcasted_iota(jnp.int32, (FR, WG), 0) < length, g_raw[...], jnp.zeros((), BF16)
    )
    gt[...] = g_all[x].T
    own_rows.core(own_half)
    count_y()
    for buf in z_sends:
        buf[...] = jnp.zeros_like(buf)
    mz_send[...] = jnp.zeros_like(mz_send)
    i_send[...] = jnp.zeros_like(i_send)
    own_rows.along_y()
    count_z()
    both_landed(a_all, ka[0:2], 0, 1)
    onward(a_all, ka[4:6])
    both(g_all, kg[0:2], None, None, near_cols)
    load_bi.wait()
    for i in range(4):
        bit[i] = bi[i * WA : (i + 1) * WA].T

    line = lax.broadcasted_iota(jnp.int32, (256, WG), 0)
    slot, at_z = line % 32, line // 32
    source = (at_z % 2) * 320 + (at_z // 2) * 40 + jnp.where(slot >= 10, 150, 0) + slot
    source = jnp.where(slot < 20, source, -WG)
    ahead = lax.broadcasted_iota(jnp.int32, (256, WG), 1) - source
    for i in range(4):
        chosen[i] = (ahead == 10 * i).astype(F32).astype(BF16)
    own_rows.along_z()
    count_done()
    both_landed(a_all, ka[2:4], 1, 0)

    def rotate_near(t, carry):
        rows = pl.ds(pl.multiple_of(t * 320, 16), 320)
        total = dot(bit[x, rows], a_all[x]) + dot(bit[left, rows], a_all[left])
        ar_part[rows] = total + dot(bit[right, rows], a_all[right])
        return carry

    lax.fori_loop(0, 4, rotate_near, 0)
    far_landed(a_all, ka[4:6])

    def cross(h):
        def rotate_far(t, carry):
            rows = pl.ds(pl.multiple_of(h * 640 + t * 320, 16), 320)
            ar[rows] = (ar_part[rows] + dot(bit[opposite, rows], a_all[opposite])).astype(BF16)
            return carry

        lax.fori_loop(0, 2, rotate_far, 0)
        return dot(ar[pl.ds(pl.multiple_of(h * 640, 16), 640)], g_all[x])

    kmc, kmy, kmz = fresh(), [fresh() for _ in range(3)], [fresh() for _ in range(7)]
    mc_send[...] = cross(1 - c).astype(BF16)
    send(mc_send, mc_recv, peer(dc=1), kmc)
    m_keep[...] = cross(c)
    both(g_all, kg[2:4], None, None, last_cols)
    landed(mc_recv, kmc)
    total = m_keep[...] + mc_recv[...].astype(F32)
    m_keep[...] = total
    my_send[...] = total.astype(BF16)
    for i in range(3):
        to = (y + i + 1) % 4
        send(
            my_send.at[pl.ds(pl.multiple_of(to * 160, 16), 160)],
            my_recv.at[i], peer(dy=i + 1), kmy[i],
        )
    in_rows.core(in_block)
    own_rows.hand_out()
    load_bo.wait()
    in_rows.along_y()
    total = m_keep[pl.ds(pl.multiple_of(y * 160, 16), 160)]
    for i in range(3):
        landed(my_recv.at[i], kmy[i])
        total = total + my_recv[i].astype(F32)
    for i in range(8):
        pieces = [total[20 * i : 20 * i + 20, 128 * j : 128 * j + 128] for j in range(5)]
        mz_send[i, :100] = jnp.concatenate(pieces, axis=0).astype(BF16)
    for i in range(7):
        send(mz_send.at[(z + i + 1) % 8], mz_recv.at[i], peer(dz=i + 1), kmz[i])
    both_landed(g_all, kg[0:2], None, None, near_cols)
    near_rows.core(near_half(near_cols))
    frames = n_total[:1, :1]
    row = lax.broadcasted_iota(jnp.int32, (32, 1280), 0) + (c * 640 + y * 160 + z * 20)
    here = lax.broadcasted_iota(jnp.int32, (32, 1280), 1) == row
    eigen_rows = jnp.concatenate([ei_ref[i : i + 1] for i in range(10)], axis=1)
    eigen_rows = jnp.sum(jnp.where(here, eigen_rows, 0.0), axis=1, keepdims=True)
    eigen_cols = jnp.concatenate([eo_ref[pl.ds(5 * x + i, 1)] for i in range(5)], axis=1)
    scale = eigen_rows * eigen_cols + damping
    total = mz_send[z].astype(F32)
    for i in range(7):
        landed(mz_recv.at[i], kmz[i])
        total = total + mz_recv[i].astype(F32)

    kmx = [fresh() for _ in range(3)]
    for j in range(5):
        mx[x, :20, 128 * j : 128 * j + 128] = total[20 * j : 20 * j + 20].astype(BF16)
    for i in range(3):
        send(mx.at[x], mx.at[x], peer(dx=i + 1), kmx[i])
    onward(g_all, kg[4:6], near_cols)
    in_rows.along_z()
    near_rows.along_y()
    both_landed(g_all, kg[2:4], None, None, last_cols)
    second_rows.core(near_half(last_cols))
    near_rows.along_z()
    for i in range(3):
        landed(mx.at[(x + 3 - i) % 4], kmx[i])
    total = jnp.zeros((32, WG), F32)
    for i in range(4):
        total = total + dot(mx[i], bo[i * WG : (i + 1) * WG])
    scaled = (total / frames / scale).astype(BF16)
    kqx, kqz = [fresh() for _ in range(3)], [fresh() for _ in range(7)]
    kqy, kqc = [fresh() for _ in range(3)], fresh()
    turned = dot_nt(scaled, bo[...]).astype(BF16)
    turned = jnp.concatenate([turned[:20, WG * i : WG * i + WG] for i in range(4)], axis=0)
    for i in range(4):
        qx_send[i] = dot_nt(turned, chosen[i]).astype(BF16)
    for i in range(3):
        send(qx_send.at[(x + i + 1) % 4], qx_recv.at[i], peer(dx=i + 1), kqx[i])
    onward(g_all, kg[6:8], last_cols)
    second_rows.along_y()
    hand_in()
    near_rows.hand_out()
    far_landed(g_all, kg[4:6], near_cols)
    far_rows.core(far_half)
    total = qx_send[x].astype(F32)
    for i in range(3):
        landed(qx_recv.at[i], kqx[i])
        total = total + qx_recv[i].astype(F32)
    for i in range(8):
        lanes = slice(32 * i, 32 * i + 32)
        pieces = [total[20 * j : 20 * j + 20, lanes] for j in range(4)]
        qz_send[i, :20] = jnp.concatenate(pieces, axis=1).astype(BF16)
    qz[z] = qz_send[z]
    for i in range(7):
        send(qz_send.at[(z + i + 1) % 8], qz.at[z], peer(dz=i + 1), kqz[i])
    second_rows.along_z()
    far_rows.along_y()
    for i in range(7):
        landed(qz.at[(z + 7 - i) % 8], kqz[i])
    for i in range(8):
        qy[y, 20 * i : 20 * i + 20] = qz[i, :20]
    for i in range(3):
        send(qy.at[y], qy.at[y], peer(dy=i + 1), kqy[i])

    far_landed(g_all, kg[6:8], last_cols)
    last_rows.core(last_half)
    far_rows.along_z()
    for i in range(3):
        landed(qy.at[(y + 3 - i) % 4], kqy[i])
    qc[c] = qy[...].reshape(640, 128)
    send(qc.at[c], qc.at[c], peer(dc=1), kqc)
    last_rows.along_y()
    second_rows.hand_out()
    far_rows.hand_out()
    last_rows.along_z()
    landed(qc.at[1 - c], kqc)
    mine = lax.broadcasted_iota(jnp.int32, (16, 128), 0) + (y * 32 + c * 10)
    mine = lax.broadcasted_iota(jnp.int32, (16, 128), 1) == mine
    picked = dot_nt(mine.astype(F32).astype(BF16), qc[...].reshape(1280, 128)).astype(BF16)
    pre_ref[...] = dot_nt(picked, bi[...])[:10].astype(BF16)

    for h in range(2):

        @pl.when(jnp.logical_not(same(in_src[h])))
        def _(h=h):
            landed(i_recv.at[h], ki[h])

        cols = slice(640 * h, 640 * h + 640)
        fin_ref[:, cols] = factor_decay * prev_in_ref[:, cols] + (1.0 - factor_decay) * (
            i_recv[h, :5] / frames
        )
    source = unit // 64

    def write_out(places, total):
        for j, (step, lane) in enumerate(places):
            at = pl.multiple_of(((source + step) % 4) * WG, 128) + lane
            lanes = pl.ds(pl.multiple_of(at, 128), 128)
            fout_ref[:, lanes] = factor_decay * prev_out_ref[:, lanes] + (1.0 - factor_decay) * (
                total[10 * j : 10 * j + 10] / frames
            )

    def tiles(step, cols=None):
        start, stop = (0, WG) if cols is None else (cols.start, cols.stop)
        return [(step, lane) for lane in range(start, stop, 128)]

    write_out(tiles(0), own_rows.handed_out())
    write_out(tiles(3, near_cols) + tiles(1, near_cols), near_rows.handed_out())
    write_out(tiles(3, last_cols) + tiles(1, last_cols), second_rows.handed_out())
    write_out(tiles(2, near_cols), far_rows.handed_out())
    write_out(tiles(2, last_cols), last_rows.done())

    for copy in started:
        copy.wait_send()
    @pl.when(jnp.logical_not(same(out_dst)))
    def _():
        for rows in (own_rows, near_rows, second_rows, far_rows):
            rows.out_copy().wait_send()

    for i in range(4):

        @pl.when(jnp.logical_not(same(turn_dsts[i])))
        def _(i=i):
            last_rows.copy(i).wait_send()

    for h in range(2):

        @pl.when(jnp.logical_not(same(in_dst[h])))
        def _(h=h):
            in_copy(h).wait_send()

    assert count[0] <= MESSAGES


def handed_on(*refs):
    for i in range(3):
        refs[3 + i][...] = refs[i][...]


def shards(
    activations, gradients, valid_frames, basis_in, basis_out, eigen_in, eigen_out,
    previous_in, previous_out,
):
    vmem = pl.BlockSpec(memory_space=pltpu.VMEM)
    hbm = pl.BlockSpec(memory_space=pl.ANY)
    V = pltpu.VMEM
    results = pl.pallas_call(
        kernel,
        out_shape=(
            jax.ShapeDtypeStruct(previous_in.shape, F32),
            jax.ShapeDtypeStruct(previous_out.shape, F32),
            jax.ShapeDtypeStruct((10, 1280), BF16),
        ),
        in_specs=[vmem, hbm, vmem, hbm, hbm, vmem, vmem, vmem, vmem],
        out_specs=(vmem, vmem, vmem),
        scratch_shapes=[
            V((4, WA, FR), BF16), V((4, FR, WG), BF16), V((WG, FR), BF16),
            V((1280, 1280), BF16), V((2560, WG), BF16), V((4, 1280, WA), BF16),
            [V((320, w), F32) for w in WIDTHS], [V((320, w), BF16) for w in WIDTHS],
            [V((320, w), BF16) for w in WIDTHS], [V((320, w), BF16) for w in WIDTHS],
            [V((4, 80, w), BF16) for w in WIDTHS], [V((8, lines_of(w), 128), BF16) for w in WIDTHS],
            [V((7, lines_of(w), 128), BF16) for w in WIDTHS],
            [V((lines_of(w), 128), F32) for w in WIDTHS], [V((lines_of(w), 128), F32) for w in WIDTHS],
            V((2, 8, 640), F32), V((2, 8, 640), F32),
            V((1280, FR), F32), V((1280, FR), BF16), V((4, 256, WG), BF16),
            V((FR, WG), BF16),
            V((640, 640), F32), V((640, 640), BF16), V((640, 640), BF16),
            V((640, 640), BF16), V((3, 160, 640), BF16),
            V((8, 112, 128), BF16), V((7, 112, 128), BF16),
            V((4, 32, 640), BF16),
            V((4, 80, 256), BF16), V((3, 80, 256), BF16), V((8, 32, 128), BF16),
            V((8, 32, 128), BF16), V((4, 160, 128), BF16), V((2, 640, 128), BF16),
            V((2, 8, 128), F32), V((4, 8, 128), F32), V((8, 8, 128), F32),
            V((8, 128), F32),
            pltpu.SemaphoreType.DMA((MESSAGES,)), pltpu.SemaphoreType.DMA((MESSAGES,)),
            pltpu.SemaphoreType.DMA((3,)),
        ],
        compiler_params=pltpu.CompilerParams(
            collective_id=0, has_side_effects=True, vmem_limit_bytes=60 * 1024 * 1024
        ),
    )(
        activations.T, gradients, valid_frames.reshape(8, 128), basis_in, basis_out,
        eigen_out.reshape(20, 128), eigen_in.reshape(10, 128), previous_in, previous_out,
    )
    return pl.pallas_call(
        handed_on,
        out_shape=[jax.ShapeDtypeStruct(r.shape, r.dtype) for r in results],
        in_specs=[vmem] * 3,
        out_specs=[vmem] * 3,
    )(*results)


def solution(mesh):
    rows = P(("tm", "dp", "factor"), None)
    in_specs = (
        P(("tm", "dp"), "factor"),
        P(("tm", "dp"), "factor"),
        P(("tm", "dp")),
        P(),
        P(None, "factor"),
        P(),
        P(),
        rows,
        rows,
    )
    return jax.shard_map(
        shards, mesh=mesh, in_specs=in_specs, out_specs=(rows, rows, rows), check_vma=False
    )
```

time: 119 us -> 103 us (0.87)
  the two profiles are of different devices: /device:TPU:1 before, /device:TPU:4 now
where the time goes in v3:
time: 103 us; the launch traced here: 102 us
  Pallas kernels  102 us (99%)
    pallas_call x1, Pallas kernels, shards(): pl.pallas_call(kernel, out_shape=(jax.ShapeDtypeStruct(previous_in.shape,...  100 us

profile of v3, /device:TPU:4, one launch (start us, length us, event | category | flops | bytes accessed | tf_op | source)
XLA Modules:
  0.0 102.4 jit_solution(13561553218412625028)
XLA Ops:
  0.6 100.1 %shard_map.112 = (f32[5,1280]{1,0:T(8,128)}, f32[10,2560]{1,0:T(8,128)}, bf16[10,1280]{1,0:T(8,128)(2,1)}) custom-call(bf16[320,1024]{1,0:T(8,128)(2,1)} %bitcast.4, bf16[1024,640]{1,0:T(8,128)(2,1)} %g_ref.1, s32[8,128]{1,0:T(8,128)} %bitcast.7, bf16[1280,1280]{1,0:T(8,128)(2,1)} %bi_ref.1, bf16[2560,640]{1,0:T(8,128)(2,1)} %bo_ref.1, f32[20,128]{1,0:T(8,128)} %bitcast.5, ...), custom_call_target="tpu_custom_call" | custom-call | tf_op jit(solution)/shard_map/pallas_call | solution.py:574
  100.8 1.6 %shard_map.113 = (f32[5,1280]{1,0:T(8,128)}, f32[10,2560]{1,0:T(8,128)}, bf16[10,1280]{1,0:T(8,128)(2,1)}) custom-call(f32[5,1280]{1,0:T(8,128)} %get-tuple-element.6.refs_0_, f32[10,2560]{1,0:T(8,128)} %get-tuple-element.7.refs_1_, bf16[10,1280]{1,0:T(8,128)(2,1)} %get-tuple-element.8.refs_2_), custom_call_target="tpu_custom_call" | custom-call | tf_op jit(solution)/shard_map/pallas_call | solution.py:612

commit v4 on v3

--- a/solution.py
+++ b/solution.py
@@ -16,7 +16,7 @@
 FR = 1024
 WA = 320
 WG = 640
-MESSAGES = 144
+MESSAGES = 80
 
 
 def device(x, y, z, c):
@@ -39,10 +39,11 @@
 
 
 def kernel(
-    at_ref, g_ref, valid_ref, bi_ref, bo_ref, eo_ref, ei_ref, prev_in_ref, prev_out_ref,
-    fin_ref, fout_ref, pre_ref,
+    at_hbm, g_hbm, valid_hbm, bi_hbm, bo_hbm, eo_hbm, ei_hbm, prev_in_hbm, prev_out_hbm,
+    fin_out, fout_out, pre_out,
     a_all, g_all, gt, bi, bo, bit,
-    keeps, c_sends, c_recvs, y_sends, y_recvs, z_sends, z_recvs, o_sends, o_recvs, i_send, i_recv,
+    keeps, c_sends, c_recvs, y_sends, y_recvs, z_sends, z_recvs, o_sends, o_recvs, l_recv, i_send, i_recv,
+    at_ref, valid_ref, eo_ref, ei_ref, prev_in_ref, prev_out_ref, fin_ref, fout_ref, pre_ref,
     ar_part, ar, chosen, g_raw, m_keep, mc_send, mc_recv, my_send, my_recv, mz_send, mz_recv, mx,
     qx_send, qx_recv, qz_send, qz, qy, qc,
     n_c, n_y, n_z, n_total,
@@ -58,6 +59,11 @@
     def peer(dx=0, dy=0, dz=0, dc=0):
         return device((x + dx) % 4, (y + dy) % 4, (z + dz) % 8, (c + dc) % 2)
 
+    out_dsts = [
+        {"tm": u // 16, "dp": (u // 4) % 4, "factor": u % 4}
+        for u in [64 * x + 32 * c + 8 * y + i for i in range(8)]
+    ]
+    out_srcs = [device(unit // 64, (unit // 8) % 4, i, (unit // 32) % 2) for i in range(8)]
     turn_dsts = [device(i, x, z, c) for i in range(4)]
     turn_srcs = [device(y, i, z, c) for i in range(4)]
     own_unit = 64 * x + 32 * c + 8 * y + z
@@ -70,34 +76,39 @@
     def same(d):
         return (d["tm"] == tm) & (d["dp"] == dp) & (d["factor"] == x)
 
-    load_bi = pltpu.make_async_copy(bi_ref, bi, load_sem.at[0])
-    load_bo = pltpu.make_async_copy(bo_ref, bo, load_sem.at[1])
-    load_g = pltpu.make_async_copy(g_ref, g_raw, load_sem.at[2])
-    load_g.start()
-    load_bi.start()
-    load_bo.start()
+    wanted = (
+        (valid_hbm, valid_ref), (at_hbm, at_ref), (g_hbm, g_raw), (bi_hbm, bi), (bo_hbm, bo),
+        (eo_hbm, eo_ref), (ei_hbm, ei_ref), (prev_in_hbm, prev_in_ref), (prev_out_hbm, prev_out_ref),
+    )
+    loads = [pltpu.make_async_copy(*pair, load_sem.at[i]) for i, pair in enumerate(wanted)]
+    load_valid, load_at, load_g, load_bi, load_bo = loads[:5]
+    load_valid.start()
+    load_at.start()
 
     barrier = pltpu.get_barrier_semaphore()
     peers = [peer(dx=i) for i in (1, 2, 3)] + [peer(dy=i) for i in (1, 2, 3)]
     peers += [peer(dz=i) for i in range(1, 8)] + [peer(dc=1)]
     for d in peers:
         pl.semaphore_signal(barrier, inc=1, device_id=d, device_id_type=MESH)
-    for d in turn_srcs + [out_src] + in_src:
+    for d in turn_srcs + out_srcs + in_src:
 
         @pl.when(jnp.logical_not(same(d)))
         def _():
             pl.semaphore_signal(barrier, inc=1, device_id=d, device_id_type=MESH)
 
     expected = len(peers)
-    for d in turn_dsts + [out_dst] + in_dst:
+    for d in turn_dsts + out_dsts + in_dst:
         expected = expected + jnp.where(same(d), 0, 1)
 
+    for load in loads[2:]:
+        load.start()
+    load_valid.wait()
+    load_at.wait()
     length = jnp.sum(valid_ref[...], keepdims=True)
     a_all[x] = jnp.where(
         lax.broadcasted_iota(jnp.int32, (WA, FR), 1) < length, at_ref[...], jnp.zeros((), BF16)
     )
     n_c[0] = jnp.broadcast_to(length.astype(F32), (8, 128))
-    mx[x] = jnp.zeros((32, WG), BF16)
     qz_send[...] = jnp.zeros_like(qz_send)
     pl.semaphore_wait(barrier, expected)
 
@@ -108,19 +119,28 @@
         count[0] += 1
         return count[0] - 1
 
-    def send(src, dst, to, k):
+    def send(src, dst, to, k, alone=True):
         copy = pltpu.make_async_remote_copy(
             src_ref=src, dst_ref=dst, send_sem=send_sem.at[k], recv_sem=recv_sem.at[k],
             device_id=to, device_id_type=MESH,
         )
         copy.start()
-        started.append(copy)
+        if alone:
+            started.append(copy)
+
+    def described(ref, k):
+        return pltpu.make_async_remote_copy(
+            src_ref=ref, dst_ref=ref, send_sem=send_sem.at[k], recv_sem=recv_sem.at[k],
+            device_id=peer(dx=1), device_id_type=MESH,
+        )
 
     def landed(dst, k):
-        pltpu.make_async_remote_copy(
-            src_ref=dst, dst_ref=dst, send_sem=send_sem.at[k], recv_sem=recv_sem.at[k],
-            device_id=peer(dx=1), device_id_type=MESH,
-        ).wait_recv()
+        described(dst, k).wait_recv()
+
+    def send_all(pairs, received, k):
+        for src, dst, to in pairs:
+            send(src, dst, to, k, alone=False)
+        started.append(described(received, k))
 
     def part(buf, shard, h, cols=None):
         rows = buf.shape[1] // 2
@@ -151,25 +171,24 @@
     both(a_all, ka[0:2], 0, 1)
     both(a_all, ka[2:4], 1, 0)
 
-    kc, ky, kz = fresh(), [fresh() for _ in range(3)], [fresh() for _ in range(7)]
+    kc, ky, kz = fresh(), fresh(), fresh()
+    n_y_others, n_z_others = n_y.at[pl.ds(1, 3)], n_z.at[pl.ds(1, 7)]
     send(n_c.at[0], n_c.at[1], peer(dc=1), kc)
 
     def count_y():
         landed(n_c.at[1], kc)
         n_y[0] = n_c[0] + n_c[1]
-        for i in range(3):
-            send(n_y.at[0], n_y.at[i + 1], peer(dy=i + 1), ky[i])
+        pairs = [(n_y.at[0], n_y.at[i + 1], peer(dy=i + 1)) for i in range(3)]
+        send_all(pairs, n_y_others, ky)
 
     def count_z():
-        for i in range(3):
-            landed(n_y.at[i + 1], ky[i])
+        landed(n_y_others, ky)
         n_z[0] = n_y[0] + n_y[1] + n_y[2] + n_y[3]
-        for i in range(7):
-            send(n_z.at[0], n_z.at[i + 1], peer(dz=i + 1), kz[i])
+        pairs = [(n_z.at[0], n_z.at[i + 1], peer(dz=i + 1)) for i in range(7)]
+        send_all(pairs, n_z_others, kz)
 
     def count_done():
-        for i in range(7):
-            landed(n_z.at[i + 1], kz[i])
+        landed(n_z_others, kz)
         total = n_z[0]
         for i in range(7):
             total = total + n_z[i + 1]
@@ -182,9 +201,8 @@
             self.y_send, self.y_recv = y_sends[b], y_recvs[b]
             self.z_send, self.z_recv = z_sends[b], z_recvs[b]
             self.o_send, self.o_recv = o_sends[b], o_recvs[b]
-            self.kc, self.ko = fresh(), fresh()
-            self.ky = [fresh() for _ in range(3)]
-            self.kz = [fresh() for _ in range(7)]
+            self.kc, self.ky, self.kz, self.ko = fresh(), fresh(), fresh(), fresh()
+            self.y_others = self.y_recv.at[pl.ds(0, 3)]
 
         def core(self, half):
             self.c_send[...] = half(1 - c).astype(BF16)
@@ -196,21 +214,20 @@
             total = self.keep[...] + self.c_recv[...].astype(F32)
             self.keep[...] = total
             self.y_send[...] = total.astype(BF16)
+            pairs = []
             for i in range(3):
-                to = (y + i + 1) % 4
-                send(
-                    self.y_send.at[pl.ds(pl.multiple_of(to * 80, 16), 80)],
-                    self.y_recv.at[i], peer(dy=i + 1), self.ky[i],
-                )
+                rows = pl.ds(pl.multiple_of((y + i + 1) % 4 * 80, 16), 80)
+                pairs.append((self.y_send.at[rows], self.y_recv.at[i], peer(dy=i + 1)))
+            send_all(pairs, self.y_others, self.ky)
 
         def sum_y(self):
             total = self.keep[pl.ds(pl.multiple_of(y * 80, 16), 80)]
+            landed(self.y_others, self.ky)
             for i in range(3):
-                landed(self.y_recv.at[i], self.ky[i])
                 total = total + self.y_recv[i].astype(F32)
             return total
 
-        def along_z(self):
+        def pack_z(self):
             total = self.sum_y()
             for i in range(8):
                 pieces = [
@@ -218,16 +235,19 @@
                 ]
                 pieces = jnp.concatenate(pieces, axis=0).astype(BF16)
                 self.z_send[i, : 10 * self.tiles] = pieces
-            for i in range(7):
-                send(
-                    self.z_send.at[(z + i + 1) % 8], self.z_recv.at[i],
-                    peer(dz=i + 1), self.kz[i],
-                )
+
+        def along_z(self):
+            self.pack_z()
+            pairs = [
+                (self.z_send.at[(z + i + 1) % 8], self.z_recv.at[i], peer(dz=i + 1))
+                for i in range(7)
+            ]
+            send_all(pairs, self.z_recv, self.kz)
 
         def done(self):
             total = self.z_send[z].astype(F32)
+            landed(self.z_recv, self.kz)
             for i in range(7):
-                landed(self.z_recv.at[i], self.kz[i])
                 total = total + self.z_recv[i].astype(F32)
             return total
 
@@ -256,16 +276,61 @@
 
             return self.o_recv[...]
 
+    class Spread:
+        def __init__(self, src, recv, slot, dsts, srcs):
+            self.src, self.recv, self.slot, self.dsts, self.srcs = src, recv, slot, dsts, srcs
+            self.k = fresh()
+            self.self_dst, self.self_src = (
+                functools.reduce(jnp.logical_or, [same(d) for d in to]) for to in (dsts, srcs)
+            )
+
+        def start(self):
+            for i, d in enumerate(self.dsts):
+
+                @pl.when(same(d))
+                def _(i=i):
+                    self.recv[self.slot] = self.src(i)[...]
+
+                @pl.when(jnp.logical_not(same(d)))
+                def _(i=i, d=d):
+                    send(self.src(i), self.recv.at[self.slot], d, self.k, alone=False)
+
+        def wait(self, own, act):
+            @pl.when(own)
+            def _():
+                act(described(self.recv.at[pl.ds(0, len(self.dsts) - 1)], self.k))
+
+            @pl.when(jnp.logical_not(own))
+            def _():
+                act(described(self.recv, self.k))
+
+        def total(self):
+            self.wait(self.self_src, lambda copy: copy.wait_recv())
+            total = self.recv[0].astype(F32)
+            for i in range(1, len(self.srcs)):
+                total = total + self.recv[i].astype(F32)
+            return total
+
+        def finish(self):
+            self.wait(self.self_dst, lambda copy: copy.wait_send())
+
+    class Straight(Scatter):
+        def __init__(self, b):
+            super().__init__(b)
+            self.spread = Spread(lambda i: self.z_send.at[i], l_recv, z, out_dsts, out_srcs)
+
+        def along_z(self):
+            self.pack_z()
+            self.spread.start()
+
+        def done(self):
+            return self.spread.total()
+
     class Turned(Scatter):
         def __init__(self, b):
             super().__init__(b)
-            self.k_send, self.k = [fresh() for _ in range(4)], [fresh() for _ in range(4)]
-
-        def copy(self, i):
-            return pltpu.make_async_remote_copy(
-                src_ref=self.y_send.at[pl.ds(80 * i, 80)], dst_ref=self.y_recv.at[y],
-                send_sem=send_sem.at[self.k_send[i]], recv_sem=recv_sem.at[self.k[0] + y],
-                device_id=turn_dsts[i], device_id_type=MESH,
+            self.spread = Spread(
+                lambda i: self.y_send.at[pl.ds(80 * i, 80)], self.y_recv, y, turn_dsts, turn_srcs
             )
 
         def along_y(self):
@@ -275,30 +340,13 @@
                 starts = [(j % 2) * 160 + (j // 2) * 40 + 10 * i for j in range(8)]
                 pieces = [total[start : start + 10] for start in starts]
                 self.y_send[80 * i : 80 * i + 80] = jnp.concatenate(pieces, axis=0).astype(BF16)
-            for i in range(4):
-                self_dst = same(turn_dsts[i])
-
-                @pl.when(self_dst)
-                def _(i=i):
-                    self.y_recv[y] = self.y_send[80 * i : 80 * i + 80]
-
-                @pl.when(jnp.logical_not(self_dst))
-                def _(i=i):
-                    self.copy(i).start()
+            self.spread.start()
 
         def sum_y(self):
-            total = jnp.zeros((80, 128 * self.tiles), F32)
-            for i in range(4):
-
-                @pl.when(jnp.logical_not(same(turn_srcs[i])))
-                def _(i=i):
-                    landed(self.y_recv.at[i], self.k[i])
-
-                total = total + self.y_recv[i].astype(F32)
-            return total
-
-    in_rows, own_rows, near_rows, second_rows, far_rows = (Scatter(i) for i in range(5))
-    last_rows = Turned(5)
+            return self.spread.total()
+
+    in_rows, own_rows, near_rows, second_rows = (Scatter(i) for i in range(4))
+    far_rows, last_rows = Straight(4), Turned(5)
     ki_send = [fresh() for _ in range(2)]
     ki = [fresh() for _ in range(2)]
 
@@ -397,7 +445,7 @@
         lax.fori_loop(0, 2, rotate_far, 0)
         return dot(ar[pl.ds(pl.multiple_of(h * 640, 16), 640)], g_all[x])
 
-    kmc, kmy, kmz = fresh(), [fresh() for _ in range(3)], [fresh() for _ in range(7)]
+    kmc, kmy, kmz, kmx, kqx = fresh(), fresh(), fresh(), [fresh() for _ in range(3)], fresh()
     mc_send[...] = cross(1 - c).astype(BF16)
     send(mc_send, mc_recv, peer(dc=1), kmc)
     m_keep[...] = cross(c)
@@ -406,42 +454,40 @@
     total = m_keep[...] + mc_recv[...].astype(F32)
     m_keep[...] = total
     my_send[...] = total.astype(BF16)
-    for i in range(3):
-        to = (y + i + 1) % 4
-        send(
-            my_send.at[pl.ds(pl.multiple_of(to * 160, 16), 160)],
-            my_recv.at[i], peer(dy=i + 1), kmy[i],
-        )
+    pairs = []
+    for i in range(3):
+        rows = pl.ds(pl.multiple_of((y + i + 1) % 4 * 160, 16), 160)
+        pairs.append((my_send.at[rows], my_recv.at[i], peer(dy=i + 1)))
+    send_all(pairs, my_recv, kmy)
     in_rows.core(in_block)
     own_rows.hand_out()
-    load_bo.wait()
+    for load in loads[4:]:
+        load.wait()
     in_rows.along_y()
     total = m_keep[pl.ds(pl.multiple_of(y * 160, 16), 160)]
-    for i in range(3):
-        landed(my_recv.at[i], kmy[i])
+    landed(my_recv, kmy)
+    for i in range(3):
         total = total + my_recv[i].astype(F32)
     for i in range(8):
         pieces = [total[20 * i : 20 * i + 20, 128 * j : 128 * j + 128] for j in range(5)]
         mz_send[i, :100] = jnp.concatenate(pieces, axis=0).astype(BF16)
-    for i in range(7):
-        send(mz_send.at[(z + i + 1) % 8], mz_recv.at[i], peer(dz=i + 1), kmz[i])
+    pairs = [(mz_send.at[(z + i + 1) % 8], mz_recv.at[i], peer(dz=i + 1)) for i in range(7)]
+    send_all(pairs, mz_recv, kmz)
     both_landed(g_all, kg[0:2], None, None, near_cols)
     near_rows.core(near_half(near_cols))
     frames = n_total[:1, :1]
-    row = lax.broadcasted_iota(jnp.int32, (32, 1280), 0) + (c * 640 + y * 160 + z * 20)
-    here = lax.broadcasted_iota(jnp.int32, (32, 1280), 1) == row
+    row = lax.broadcasted_iota(jnp.int32, (20, 1280), 0) + (c * 640 + y * 160 + z * 20)
+    here = lax.broadcasted_iota(jnp.int32, (20, 1280), 1) == row
     eigen_rows = jnp.concatenate([ei_ref[i : i + 1] for i in range(10)], axis=1)
     eigen_rows = jnp.sum(jnp.where(here, eigen_rows, 0.0), axis=1, keepdims=True)
     eigen_cols = jnp.concatenate([eo_ref[pl.ds(5 * x + i, 1)] for i in range(5)], axis=1)
     scale = eigen_rows * eigen_cols + damping
     total = mz_send[z].astype(F32)
+    landed(mz_recv, kmz)
     for i in range(7):
-        landed(mz_recv.at[i], kmz[i])
         total = total + mz_recv[i].astype(F32)
 
-    kmx = [fresh() for _ in range(3)]
-    for j in range(5):
-        mx[x, :20, 128 * j : 128 * j + 128] = total[20 * j : 20 * j + 20].astype(BF16)
+    mx[x] = total.astype(BF16)
     for i in range(3):
         send(mx.at[x], mx.at[x], peer(dx=i + 1), kmx[i])
     onward(g_all, kg[4:6], near_cols)
@@ -452,18 +498,19 @@
     near_rows.along_z()
     for i in range(3):
         landed(mx.at[(x + 3 - i) % 4], kmx[i])
-    total = jnp.zeros((32, WG), F32)
+    total = jnp.zeros((20, WG), F32)
     for i in range(4):
-        total = total + dot(mx[i], bo[i * WG : (i + 1) * WG])
+        pieces = [mx[i, 20 * j : 20 * j + 20] for j in range(5)]
+        total = total + dot(jnp.concatenate(pieces, axis=1), bo[i * WG : (i + 1) * WG])
     scaled = (total / frames / scale).astype(BF16)
-    kqx, kqz = [fresh() for _ in range(3)], [fresh() for _ in range(7)]
+    kqz = [fresh() for _ in range(7)]
     kqy, kqc = [fresh() for _ in range(3)], fresh()
     turned = dot_nt(scaled, bo[...]).astype(BF16)
-    turned = jnp.concatenate([turned[:20, WG * i : WG * i + WG] for i in range(4)], axis=0)
+    turned = jnp.concatenate([turned[:, WG * i : WG * i + WG] for i in range(4)], axis=0)
     for i in range(4):
         qx_send[i] = dot_nt(turned, chosen[i]).astype(BF16)
-    for i in range(3):
-        send(qx_send.at[(x + i + 1) % 4], qx_recv.at[i], peer(dx=i + 1), kqx[i])
+    pairs = [(qx_send.at[(x + i + 1) % 4], qx_recv.at[i], peer(dx=i + 1)) for i in range(3)]
+    send_all(pairs, qx_recv, kqx)
     onward(g_all, kg[6:8], last_cols)
     second_rows.along_y()
     hand_in()
@@ -471,8 +518,8 @@
     far_landed(g_all, kg[4:6], near_cols)
     far_rows.core(far_half)
     total = qx_send[x].astype(F32)
-    for i in range(3):
-        landed(qx_recv.at[i], kqx[i])
+    landed(qx_recv, kqx)
+    for i in range(3):
         total = total + qx_recv[i].astype(F32)
     for i in range(8):
         lanes = slice(32 * i, 32 * i + 32)
@@ -483,29 +530,32 @@
         send(qz_send.at[(z + i + 1) % 8], qz.at[z], peer(dz=i + 1), kqz[i])
     second_rows.along_z()
     far_rows.along_y()
+    far_landed(g_all, kg[6:8], last_cols)
+    last_rows.core(last_half)
     for i in range(7):
         landed(qz.at[(z + 7 - i) % 8], kqz[i])
     for i in range(8):
         qy[y, 20 * i : 20 * i + 20] = qz[i, :20]
     for i in range(3):
         send(qy.at[y], qy.at[y], peer(dy=i + 1), kqy[i])
-
-    far_landed(g_all, kg[6:8], last_cols)
-    last_rows.core(last_half)
+    second_rows.hand_out()
+    last_rows.along_y()
     far_rows.along_z()
     for i in range(3):
         landed(qy.at[(y + 3 - i) % 4], kqy[i])
     qc[c] = qy[...].reshape(640, 128)
     send(qc.at[c], qc.at[c], peer(dc=1), kqc)
-    last_rows.along_y()
-    second_rows.hand_out()
-    far_rows.hand_out()
     last_rows.along_z()
     landed(qc.at[1 - c], kqc)
     mine = lax.broadcasted_iota(jnp.int32, (16, 128), 0) + (y * 32 + c * 10)
     mine = lax.broadcasted_iota(jnp.int32, (16, 128), 1) == mine
     picked = dot_nt(mine.astype(F32).astype(BF16), qc[...].reshape(1280, 128)).astype(BF16)
     pre_ref[...] = dot_nt(picked, bi[...])[:10].astype(BF16)
+    stores = [
+        pltpu.make_async_copy(pair[0], pair[1], load_sem.at[9 + i])
+        for i, pair in enumerate(((pre_ref, pre_out), (fin_ref, fin_out), (fout_ref, fout_out)))
+    ]
+    stores[0].start()
 
     for h in range(2):
 
@@ -517,6 +567,7 @@
         fin_ref[:, cols] = factor_decay * prev_in_ref[:, cols] + (1.0 - factor_decay) * (
             i_recv[h, :5] / frames
         )
+    stores[1].start()
     source = unit // 64
 
     def write_out(places, total):
@@ -534,29 +585,28 @@
     write_out(tiles(0), own_rows.handed_out())
     write_out(tiles(3, near_cols) + tiles(1, near_cols), near_rows.handed_out())
     write_out(tiles(3, last_cols) + tiles(1, last_cols), second_rows.handed_out())
-    write_out(tiles(2, near_cols), far_rows.handed_out())
+    write_out(tiles(2, near_cols), far_rows.done())
     write_out(tiles(2, last_cols), last_rows.done())
+    stores[2].start()
 
     for copy in started:
         copy.wait_send()
     @pl.when(jnp.logical_not(same(out_dst)))
     def _():
-        for rows in (own_rows, near_rows, second_rows, far_rows):
+        for rows in (own_rows, near_rows, second_rows):
             rows.out_copy().wait_send()
 
-    for i in range(4):
-
-        @pl.when(jnp.logical_not(same(turn_dsts[i])))
-        def _(i=i):
-            last_rows.copy(i).wait_send()
-
+    far_rows.spread.finish()
+    last_rows.spread.finish()
     for h in range(2):
 
         @pl.when(jnp.logical_not(same(in_dst[h])))
         def _(h=h):
             in_copy(h).wait_send()
 
-    assert count[0] <= MESSAGES
+    for store in stores:
+        store.wait()
+    assert count[0] <= MESSAGES, count[0]
 
 
 def handed_on(*refs):
@@ -578,8 +628,8 @@
             jax.ShapeDtypeStruct(previous_out.shape, F32),
             jax.ShapeDtypeStruct((10, 1280), BF16),
         ),
-        in_specs=[vmem, hbm, vmem, hbm, hbm, vmem, vmem, vmem, vmem],
-        out_specs=(vmem, vmem, vmem),
+        in_specs=[hbm] * 9,
+        out_specs=(hbm, hbm, hbm),
         scratch_shapes=[
             V((4, WA, FR), BF16), V((4, FR, WG), BF16), V((WG, FR), BF16),
             V((1280, 1280), BF16), V((2560, WG), BF16), V((4, 1280, WA), BF16),
@@ -588,19 +638,22 @@
             [V((4, 80, w), BF16) for w in WIDTHS], [V((8, lines_of(w), 128), BF16) for w in WIDTHS],
             [V((7, lines_of(w), 128), BF16) for w in WIDTHS],
             [V((lines_of(w), 128), F32) for w in WIDTHS], [V((lines_of(w), 128), F32) for w in WIDTHS],
-            V((2, 8, 640), F32), V((2, 8, 640), F32),
+            V((8, lines_of(WIDTHS[4]), 128), BF16), V((2, 8, 640), F32), V((2, 8, 640), F32),
+            V((WA, FR), BF16), V((8, 128), jnp.int32), V((20, 128), F32), V((10, 128), F32),
+            V((5, 1280), F32), V((10, 2560), F32),
+            V((5, 1280), F32), V((10, 2560), F32), V((10, 1280), BF16),
             V((1280, FR), F32), V((1280, FR), BF16), V((4, 256, WG), BF16),
             V((FR, WG), BF16),
             V((640, 640), F32), V((640, 640), BF16), V((640, 640), BF16),
             V((640, 640), BF16), V((3, 160, 640), BF16),
             V((8, 112, 128), BF16), V((7, 112, 128), BF16),
-            V((4, 32, 640), BF16),
+            V((4, 112, 128), BF16),
             V((4, 80, 256), BF16), V((3, 80, 256), BF16), V((8, 32, 128), BF16),
             V((8, 32, 128), BF16), V((4, 160, 128), BF16), V((2, 640, 128), BF16),
             V((2, 8, 128), F32), V((4, 8, 128), F32), V((8, 8, 128), F32),
             V((8, 128), F32),
             pltpu.SemaphoreType.DMA((MESSAGES,)), pltpu.SemaphoreType.DMA((MESSAGES,)),
-            pltpu.SemaphoreType.DMA((3,)),
+            pltpu.SemaphoreType.DMA((12,)),
         ],
         compiler_params=pltpu.CompilerParams(
             collective_id=0, has_side_effects=True, vmem_limit_bytes=60 * 1024 * 1024

time: 103 us -> 98.8 us (0.959)
  the two profiles are of different devices: /device:TPU:4 before, /device:TPU:1 now
where the time goes in v4:
time: 98.8 us; the launch traced here: 98.7 us
  Pallas kernels  98 us (99%)
    pallas_call x1, Pallas kernels, shards(): pl.pallas_call(kernel, out_shape=(jax.ShapeDtypeStruct(previous_in.shape,...  96.4 us

profile of v4, /device:TPU:1, one launch (start us, length us, event | category | flops | bytes accessed | tf_op | source)
XLA Modules:
  0.0 98.7 jit_solution(1326224415198566279)
XLA Ops:
  0.6 96.4 %shard_map.112 = (f32[5,1280]{1,0:T(8,128)}, f32[10,2560]{1,0:T(8,128)}, bf16[10,1280]{1,0:T(8,128)(2,1)}) custom-call(bf16[320,1024]{1,0:T(8,128)(2,1)} %bitcast.4, bf16[1024,640]{1,0:T(8,128)(2,1)} %g_hbm.1, s32[8,128]{1,0:T(8,128)} %bitcast.7, bf16[1280,1280]{1,0:T(8,128)(2,1)} %bi_hbm.1, bf16[2560,640]{1,0:T(8,128)(2,1)} %bo_hbm.1, f32[20,128]{1,0:T(8,128)} %bitcast.5, ...), custom_call_target="tpu_custom_call" | custom-call | tf_op jit(solution)/shard_map/pallas_call | solution.py:624
  97.0 1.6 %shard_map.113 = (f32[5,1280]{1,0:T(8,128)}, f32[10,2560]{1,0:T(8,128)}, bf16[10,1280]{1,0:T(8,128)(2,1)}) custom-call(f32[5,1280]{1,0:T(8,128)} %get-tuple-element.6.refs_0_, f32[10,2560]{1,0:T(8,128)} %get-tuple-element.7.refs_1_, bf16[10,1280]{1,0:T(8,128)(2,1)} %get-tuple-element.8.refs_2_), custom_call_target="tpu_custom_call" | custom-call | tf_op jit(solution)/shard_map/pallas_call | solution.py:665

commit v5 on v4

--- a/solution.py
+++ b/solution.py
@@ -16,7 +16,7 @@
 FR = 1024
 WA = 320
 WG = 640
-MESSAGES = 80
+MESSAGES = 65
 
 
 def device(x, y, z, c):
@@ -31,7 +31,7 @@
     return lax.dot_general(left, right, (((1,), (1,)), ((), ())), preferred_element_type=F32)
 
 
-WIDTHS = (640, 640, 768, 512, 384, 256)
+WIDTHS = (640, 640, 1024, 256, 512, 128)
 
 
 def lines_of(width):
@@ -149,7 +149,7 @@
 
     ka = [fresh() for _ in range(6)]
     kg = [fresh() for _ in range(8)]
-    near_cols, last_cols = slice(0, 384), slice(384, 640)
+    near_cols, last_cols = slice(0, 512), slice(512, 640)
 
     def both(buf, k, to_right, to_left, cols=None):
         for shard, h, i in ((x, to_right, 1), (x, to_left, 3)):

time: 98.8 us -> 97.9 us (level)
  no operation moved by 1% of the time
where the time goes in v5:
time: 97.9 us; the launch traced here: 97.8 us
  Pallas kernels  97.2 us (99%)
    pallas_call x1, Pallas kernels, shards(): pl.pallas_call(kernel, out_shape=(jax.ShapeDtypeStruct(previous_in.shape,...  95.6 us

profile of v5, /device:TPU:1, one launch (start us, length us, event | category | flops | bytes accessed | tf_op | source)
XLA Modules:
  0.0 97.8 jit_solution(16073460737643897999)
XLA Ops:
  0.6 95.6 %shard_map.112 = (f32[5,1280]{1,0:T(8,128)}, f32[10,2560]{1,0:T(8,128)}, bf16[10,1280]{1,0:T(8,128)(2,1)}) custom-call(bf16[320,1024]{1,0:T(8,128)(2,1)} %bitcast.4, bf16[1024,640]{1,0:T(8,128)(2,1)} %g_hbm.1, s32[8,128]{1,0:T(8,128)} %bitcast.7, bf16[1280,1280]{1,0:T(8,128)(2,1)} %bi_hbm.1, bf16[2560,640]{1,0:T(8,128)(2,1)} %bo_hbm.1, f32[20,128]{1,0:T(8,128)} %bitcast.5, ...), custom_call_target="tpu_custom_call" | custom-call | tf_op jit(solution)/shard_map/pallas_call | solution.py:624
  96.2 1.6 %shard_map.113 = (f32[5,1280]{1,0:T(8,128)}, f32[10,2560]{1,0:T(8,128)}, bf16[10,1280]{1,0:T(8,128)(2,1)}) custom-call(f32[5,1280]{1,0:T(8,128)} %get-tuple-element.6.refs_0_, f32[10,2560]{1,0:T(8,128)} %get-tuple-element.7.refs_1_, bf16[10,1280]{1,0:T(8,128)(2,1)} %get-tuple-element.8.refs_2_), custom_call_target="tpu_custom_call" | custom-call | tf_op jit(solution)/shard_map/pallas_call | solution.py:665

commit v6 on v5

--- a/solution.py
+++ b/solution.py
@@ -539,8 +539,8 @@
     for i in range(3):
         send(qy.at[y], qy.at[y], peer(dy=i + 1), kqy[i])
     second_rows.hand_out()
+    far_rows.along_z()
     last_rows.along_y()
-    far_rows.along_z()
     for i in range(3):
         landed(qy.at[(y + 3 - i) % 4], kqy[i])
     qc[c] = qy[...].reshape(640, 128)

time: 97.9 us -> 99.7 us (1.018); the launches traced: 97.8 us -> 98.4 us
  no operation moved by 1% of the time
where the time goes in v6:
time: 99.7 us; the launch traced here: 98.4 us
  Pallas kernels  97.7 us (98%)
    pallas_call x1, Pallas kernels, shards(): pl.pallas_call(kernel, out_shape=(jax.ShapeDtypeStruct(previous_in.shape,...  96.1 us

profile of v6, /device:TPU:1, one launch (start us, length us, event | category | flops | bytes accessed | tf_op | source)
XLA Modules:
  0.0 98.4 jit_solution(12797718022156059019)
XLA Ops:
  0.6 96.1 %shard_map.112 = (f32[5,1280]{1,0:T(8,128)}, f32[10,2560]{1,0:T(8,128)}, bf16[10,1280]{1,0:T(8,128)(2,1)}) custom-call(bf16[320,1024]{1,0:T(8,128)(2,1)} %bitcast.4, bf16[1024,640]{1,0:T(8,128)(2,1)} %g_hbm.1, s32[8,128]{1,0:T(8,128)} %bitcast.7, bf16[1280,1280]{1,0:T(8,128)(2,1)} %bi_hbm.1, bf16[2560,640]{1,0:T(8,128)(2,1)} %bo_hbm.1, f32[20,128]{1,0:T(8,128)} %bitcast.5, ...), custom_call_target="tpu_custom_call" | custom-call | tf_op jit(solution)/shard_map/pallas_call | solution.py:624
  96.8 1.6 %shard_map.113 = (f32[5,1280]{1,0:T(8,128)}, f32[10,2560]{1,0:T(8,128)}, bf16[10,1280]{1,0:T(8,128)(2,1)}) custom-call(f32[5,1280]{1,0:T(8,128)} %get-tuple-element.6.refs_0_, f32[10,2560]{1,0:T(8,128)} %get-tuple-element.7.refs_1_, bf16[10,1280]{1,0:T(8,128)(2,1)} %get-tuple-element.8.refs_2_), custom_call_target="tpu_custom_call" | custom-call | tf_op jit(solution)/shard_map/pallas_call | solution.py:665
